TPU v7x, 32 devices: a whole 2x2x4 slice. The times are simulated.
32 devices in a mesh: expert: 4 (over y, x), context: 4 (over z), tensor: 2 (over core).
Axes of the slice: x: 2, y: 2, z: 4, core: 2. Of those that a mesh axis runs over, the one named last changes fastest.
Arguments:
- queries: bfloat16 [2048, 2048], P(('expert', 'context'), 'tensor'), may hold values from -6 to 6
- key_input: bfloat16 [2048, 2048], P(('expert', 'context'), 'tensor'), may hold values from -6 to 6
- value_input: bfloat16 [2048, 2048], P(('expert', 'context'), 'tensor'), may hold values from -6 to 6
- residual: bfloat16 [2048, 2048], P(('expert', 'context'), 'tensor'), may hold values from -40 to 40
- grad_output: bfloat16 [2048, 2048], P(('expert', 'context'), 'tensor'), may hold values from -6 to 6
- expert_of: int32 [2048, 1], P(('expert', 'context')), may hold values from 0 to 7; in each aligned block of 128 rows (0 to 127, 128 to 255, ...) at most 18 rows name the same one
- gate_weight: bfloat16 [8, 2048, 4096], P(('expert', 'tensor'), None, 'context'), may hold values from -0.125 to 0.125
- up_weight: bfloat16 [8, 2048, 4096], P(('expert', 'tensor'), None, 'context'), may hold values from -0.125 to 0.125
- down_weight: bfloat16 [8, 4096, 2048], P(('expert', 'tensor'), 'context'), may hold values from -0.09375 to 0.09375
Outputs:
- grad_queries: bfloat16 [2048, 2048], P(('expert', 'context'), 'tensor')
- grad_keys: bfloat16 [2048, 2048], P(('expert', 'context'), 'tensor')
- grad_values: bfloat16 [2048, 2048], P(('expert', 'context'), 'tensor')
- grad_residual: bfloat16 [2048, 2048], P(('expert', 'context'), 'tensor')
- grad_gate: bfloat16 [8, 2048, 4096], P(('expert', 'tensor'), None, 'context')
- grad_up: bfloat16 [8, 2048, 4096], P(('expert', 'tensor'), None, 'context')
- grad_down: bfloat16 [8, 4096, 2048], P(('expert', 'tensor'), 'context')
Inputs may be any that keep to these rules, and one draw needn't show every extreme that they name: `expert_of`: in each aligned block of 128 rows (the rows of one device) no expert is named by more than 18 rows, and 18 is reached in some block.
All inputs are finite; a program needn't handle non-finite values.
Results may differ from a plain program's by a relative error of at most 0.011.
Values may be sent and summed in bfloat16 or wider, within the bound.
A program may use at most 192 MiB of HBM per device.

v0:
```python
import jax
import jax.numpy as jnp
from jax import lax
from jax.sharding import PartitionSpec as P

HD = 128


EPSILON = 1e-06


def widen(array):
    return lax.optimization_barrier(array).astype(jnp.float32)


def masked_scores(query_heads, key_heads, query_start, score_scale):
    scores = (
        jnp.einsum("qhd,khd->hqk", query_heads, key_heads, preferred_element_type=jnp.float32)
        * score_scale
    )
    query_pos = query_start + jnp.arange(query_heads.shape[0], dtype=jnp.int32)
    key_pos = jnp.arange(key_heads.shape[0], dtype=jnp.int32)
    causal = key_pos[None, :] <= query_pos[:, None]
    return jnp.where(causal[None], scores, -jnp.inf)


def on_device(
    queries,
    key_input,
    value_input,
    residual,
    grad_output,
    expert_of,
    gate_weight,
    up_weight,
    down_weight,
):
    row_count = queries.shape[0]
    head_count = queries.shape[1] // HD
    n_expert = lax.axis_size("expert")
    n_tensor = lax.axis_size("tensor")
    features = queries.shape[1] * n_tensor
    score_scale = HD ** (-0.5)
    own_start = lax.axis_index("context") * row_count
    own_parity = lax.axis_index("tensor")
    all_keys, all_values = (
        lax.all_gather(key_input, "context", axis=0, tiled=True),
        lax.all_gather(value_input, "context", axis=0, tiled=True),
    )
    length = all_keys.shape[0]
    query_heads = queries.reshape(row_count, head_count, HD)
    key_heads = all_keys.reshape(length, head_count, HD)
    value_heads = all_values.reshape(length, head_count, HD)
    scores = masked_scores(query_heads, key_heads, own_start, score_scale)
    row_max = jnp.max(scores, axis=-1, keepdims=True)
    shifted = jnp.exp(scores - row_max)
    row_total = jnp.sum(shifted, axis=-1, keepdims=True)
    attn_probs = (shifted / row_total).astype(jnp.bfloat16)
    attn = jnp.einsum("hqk,khd->qhd", attn_probs, value_heads, preferred_element_type=jnp.float32)
    attn = attn.astype(jnp.bfloat16).reshape(row_count, -1)
    state = residual.astype(jnp.float32) + widen(attn)
    total_sq = lax.psum(jnp.sum(state * state, axis=-1), "tensor")
    inv_rms = (1.0 / jnp.sqrt(total_sq / features + EPSILON))[:, None]
    normed_exact = state * inv_rms
    normed = normed_exact.astype(jnp.bfloat16)
    n_all = n_expert * n_tensor
    capacity = row_count // n_all + max(1, row_count // (8 * n_all))
    expert_ids = expert_of[:, 0]
    onehot = (expert_ids[:, None] == jnp.arange(n_all, dtype=jnp.int32)[None, :]).astype(jnp.int32)
    earlier = jnp.cumsum(onehot, axis=0) - onehot
    slot_of = jnp.sum(earlier * onehot, axis=1)
    mine = expert_ids % n_tensor == own_parity
    target = jnp.where(mine, expert_ids // n_tensor * capacity + slot_of, n_expert * capacity)
    placing = (target[None, :] == jnp.arange(n_expert * capacity, dtype=jnp.int32)[:, None]).astype(
        jnp.bfloat16
    )
    full_normed, full_grad = (
        lax.all_gather(normed, "tensor", axis=1, tiled=True),
        lax.all_gather(grad_output, "tensor", axis=1, tiled=True),
    )
    send_normed = jnp.dot(placing, full_normed, preferred_element_type=jnp.float32).astype(
        jnp.bfloat16
    )
    send_grad = jnp.dot(placing, full_grad, preferred_element_type=jnp.float32).astype(jnp.bfloat16)
    send_normed = send_normed.reshape(n_expert, capacity, -1)
    send_grad = send_grad.reshape(n_expert, capacity, -1)
    got_normed, got_grad = (
        lax.all_to_all(send_normed, "expert", split_axis=0, concat_axis=0, tiled=True),
        lax.all_to_all(send_grad, "expert", split_axis=0, concat_axis=0, tiled=True),
    )
    routed_normed, routed_grad = (
        lax.all_gather(got_normed[None], "context", axis=0, tiled=True),
        lax.all_gather(got_grad[None], "context", axis=0, tiled=True),
    )
    routed_normed = routed_normed.reshape(-1, features)
    routed_grad = routed_grad.reshape(-1, features)
    gate_local = gate_weight[0]
    up_local = up_weight[0]
    down_local = down_weight[0]
    gate = jnp.dot(routed_normed, gate_local, preferred_element_type=jnp.float32)
    up_value = jnp.dot(routed_normed, up_local, preferred_element_type=jnp.float32)
    sigmoid_gate = jax.nn.sigmoid(gate)
    activation = (gate * sigmoid_gate * up_value).astype(jnp.bfloat16)
    grad_act = jnp.einsum("rd,fd->rf", routed_grad, down_local, preferred_element_type=jnp.float32)
    grad_gate_rows = (
        grad_act * up_value * sigmoid_gate * (1.0 + gate * (1.0 - sigmoid_gate))
    ).astype(jnp.bfloat16)
    grad_up_rows = (grad_act * gate * sigmoid_gate).astype(jnp.bfloat16)
    grad_down = jnp.dot(activation.T, routed_grad, preferred_element_type=jnp.float32).astype(
        jnp.bfloat16
    )[None]
    grad_gate = jnp.dot(routed_normed.T, grad_gate_rows, preferred_element_type=jnp.float32).astype(
        jnp.bfloat16
    )[None]
    grad_up = jnp.dot(routed_normed.T, grad_up_rows, preferred_element_type=jnp.float32).astype(
        jnp.bfloat16
    )[None]
    term = jnp.einsum("rf,df->rd", grad_gate_rows, gate_local, preferred_element_type=jnp.float32)
    summed_rows = lax.psum_scatter(
        term + jnp.einsum("rf,df->rd", grad_up_rows, up_local, preferred_element_type=jnp.float32),
        "context",
        scatter_dimension=0,
        tiled=True,
    )
    returned = lax.all_to_all(
        summed_rows.reshape(n_expert, capacity, -1),
        "expert",
        split_axis=0,
        concat_axis=0,
        tiled=True,
    )
    padded = jnp.concatenate(
        [returned.reshape(n_expert * capacity, -1), jnp.zeros((1, features), jnp.float32)], axis=0
    )
    full_grad_normed = jnp.take(padded, target, axis=0)
    grad_normed = lax.psum_scatter(full_grad_normed, "tensor", scatter_dimension=1, tiled=True)
    inner_sum = lax.psum(jnp.sum(normed_exact * grad_normed, axis=-1), "tensor")
    grad_state = grad_output.astype(jnp.float32) + inv_rms * (
        grad_normed - normed_exact * (inner_sum / features)[:, None]
    )
    grad_residual = grad_state.astype(jnp.bfloat16)
    grad_heads = grad_residual.reshape(row_count, head_count, HD)
    grad_probs = jnp.einsum(
        "qhd,khd->hqk", grad_heads, value_heads, preferred_element_type=jnp.float32
    )
    probs_exact = widen(attn_probs)
    row_dot = jnp.sum(probs_exact * grad_probs, axis=-1, keepdims=True)
    grad_scores = (probs_exact * (grad_probs - row_dot) * score_scale).astype(jnp.bfloat16)
    grad_queries = jnp.einsum(
        "hqk,khd->qhd", grad_scores, key_heads, preferred_element_type=jnp.float32
    )
    grad_queries = grad_queries.astype(jnp.bfloat16).reshape(row_count, -1)
    key_part = jnp.einsum(
        "hqk,qhd->khd", grad_scores, query_heads, preferred_element_type=jnp.float32
    )
    value_part = jnp.einsum(
        "hqk,qhd->khd", attn_probs, grad_heads, preferred_element_type=jnp.float32
    )
    combined = lax.psum_scatter(
        jnp.concatenate(
            [
                key_part.reshape(lax.axis_size("context") * row_count, -1),
                value_part.reshape(lax.axis_size("context") * row_count, -1),
            ],
            axis=1,
        ),
        "context",
        scatter_dimension=0,
        tiled=True,
    )
    split_at = combined.shape[1] // 2
    grad_keys = combined[:, :split_at].astype(jnp.bfloat16)
    grad_values = combined[:, split_at:].astype(jnp.bfloat16)
    return (grad_queries, grad_keys, grad_values, grad_residual, grad_gate, grad_up, grad_down)


def solution(mesh):
    return jax.shard_map(
        on_device,
        mesh=mesh,
        in_specs=(
            P(("expert", "context"), "tensor"),
            P(("expert", "context"), "tensor"),
            P(("expert", "context"), "tensor"),
            P(("expert", "context"), "tensor"),
            P(("expert", "context"), "tensor"),
            P(("expert", "context"), None),
            P(("expert", "tensor"), None, "context"),
            P(("expert", "tensor"), None, "context"),
            P(("expert", "tensor"), "context", None),
        ),
        out_specs=(
            P(("expert", "context"), "tensor"),
            P(("expert", "context"), "tensor"),
            P(("expert", "context"), "tensor"),
            P(("expert", "context"), "tensor"),
            P(("expert", "tensor"), None, "context"),
            P(("expert", "tensor"), None, "context"),
            P(("expert", "tensor"), "context", None),
        ),
        check_vma=False,
    )
```

profile of v0, /device:TPU:0, one launch (start us, length us, event | category | flops | bytes accessed | tf_op | source)
XLA Modules:
  0.0 351.5 jit_solution(13490354645173984249)
XLA Ops:
  7.2 1.8 copy.39
  9.1 0.7 all-gather.9.cloned.1.call-update
  9.8 0.7 fusion.32
  10.6 0.2 reduce_window_sum.11
  10.8 0.8 select_reduce_fusion
  11.6 2.5 all_gather.20
  14.1 0.2 convolution_convert_fusion.1
  14.3 0.8 reshape.148
  15.2 5.1 %all-to-all-start = ((bf16[4,18,2048]{2,1,0:T(8,128)(2,1)}), bf16[4,18,2048]{2,1,0:T(8,128)(2,1)S(1)}, u32[]{:S(2)}, u32[]{:S(2)}) async-start(bf16[4,18,2048]{2,1,0:T(8,128)(2,1)} %reshape.148), calls=%async_computation | async-start | bytes 786432 | tf_op jit(solution)/shard_map/all_to_all | solution.py:89
  20.6 6.6 %all-to-all-done = bf16[4,18,2048]{2,1,0:T(8,128)(2,1)S(1)} async-done(((bf16[4,18,2048]{2,1,0:T(8,128)(2,1)}), bf16[4,18,2048]{2,1,0:T(8,128)(2,1)S(1)}, u32[]{:S(2)}, u32[]{:S(2)}) %all-to-all-start) | async-done | bytes 294944 | tf_op jit(solution)/shard_map/all_to_all | solution.py:89
  27.2 0.7 copy-done.1
  28.0 15.1 %all-gather.7.cloned.1.call-done = bf16[512,1024]{0,1:T(8,128)(2,1)} async-done(((bf16[128,1024]{0,1:T(8,128)(2,1)}), bf16[512,1024]{0,1:T(8,128)(2,1)}) %all-gather.7.cloned.1.call-update) | async-done | bytes 1048592 | tf_op jit(solution)/shard_map/all_gather | solution.py:47
  43.1 3.4 fusion.43
  46.5 24.4 %all-gather.9.cloned.1.call-done = bf16[512,1024]{1,0:T(8,128)(2,1)} async-done(((bf16[128,1024]{1,0:T(8,128)(2,1)}), bf16[512,1024]{1,0:T(8,128)(2,1)}) %all-gather.9.cloned.1.call-update) | async-done | bytes 1048592 | tf_op jit(solution)/shard_map/all_gather | solution.py:48
  71.0 1.5 copy.42
  72.5 1.8 divide_convert_fusion
  74.3 0.4 convolution_convert_fusion.2
  74.9 0.4 copy-done
  75.4 2.5 psum.14
  78.0 2.2 all_gather.22
  80.2 0.9 convolution_convert_fusion
  81.1 1.1 reshape.150
  82.2 11.0 %all_to_all.15 = bf16[4,18,2048]{2,1,0:T(8,128)(2,1)} all-to-all(bf16[4,18,2048]{2,1,0:T(8,128)(2,1)S(1)} %reshape.150), channel_id=1, replica_groups=mesh['expert'=4,'context'=4,'tensor'=2] {'expert'}, dimensions={0} | all-to-all | bytes 589824 | tf_op jit(solution)/shard_map/all_to_all | solution.py:88
  93.3 16.5 %all-gather.11.cloned.1.call-done = bf16[16,18,2048]{2,1,0:T(8,128)(2,1)} async-done(((bf16[4,18,2048]{2,1,0:T(8,128)(2,1)}), bf16[16,18,2048]{2,1,0:T(8,128)(2,1)}) %all-gather.11.cloned.1.call-update) | async-done | bytes 1179664 | tf_op jit(solution)/shard_map/all_gather | solution.py:93
  109.7 2.4 reshape.149
  112.1 35.0 %all-gather.13.cloned.1.call-done = bf16[16,18,2048]{2,1,0:T(8,128)(2,1)} async-done(((bf16[4,18,2048]{2,1,0:T(8,128)(2,1)}), bf16[16,18,2048]{2,1,0:T(8,128)(2,1)}) %all-gather.13.cloned.1.call-update) | async-done | bytes 1179664 | tf_op jit(solution)/shard_map/all_gather | solution.py:92
  147.1 2.4 reshape.151
  149.5 4.1 %fusion.4 = f32[288,1024]{1,0:T(8,128)S(1)} fusion(bf16[288,2048]{1,0:T(8,128)(2,1)} %reshape.151, bf16[1,2048,1024]{2,1,0:T(8,128)(2,1)} %param.15), kind=kOutput, calls=%fused_computation.6 | convolution fusion | flops 1207959552 | bytes 6553600 | tf_op jit(solution)/shard_map/dot_general | solution.py:100
  153.7 1.4 fusion.8
  155.1 0.3 copy-done.2
  155.3 1.3 copy-done.11
  156.6 1.8 multiply_convert_fusion.1
  158.4 0.8 copy-done.12
  159.2 1.4 fusion.2
  160.7 2.8 fusion.12
  163.5 47.0 %reduce-scatter.4.cloned.1.call-done = f32[72,2048]{1,0:T(8,128)} async-done(((f32[288,2048]{1,0:T(8,128)}), f32[72,2048]{1,0:T(8,128)}) %reduce-scatter.4.cloned.1.call-update) | async-done | bytes 589840 | tf_op jit(solution)/shard_map/reduce_scatter | solution.py:119
  210.6 2.0 reshape.152
  212.6 4.2 %all-to-all-start.2 = ((f32[4,18,2048]{2,1,0:T(8,128)}), f32[4,18,2048]{2,1,0:T(8,128)}, u32[]{:S(2)}, u32[]{:S(2)}) async-start(f32[4,18,2048]{2,1,0:T(8,128)} %reshape.152), calls=%async_computation.3 | async-start | bytes 1572864 | tf_op jit(solution)/shard_map/all_to_all | solution.py:125
  216.9 10.9 %all-to-all-done.2 = f32[4,18,2048]{2,1,0:T(8,128)} async-done(((f32[4,18,2048]{2,1,0:T(8,128)}), f32[4,18,2048]{2,1,0:T(8,128)}, u32[]{:S(2)}, u32[]{:S(2)}) %all-to-all-start.2) | async-done | bytes 589856 | tf_op jit(solution)/shard_map/all_to_all | solution.py:125
  227.8 2.0 reshape.153
  229.9 1.1 concatenate.6
  231.0 1.9 gather_fusion
  232.9 2.4 broadcast_select_fusion
  235.3 0.2 reduce-scatter.8.cloned.1.call-start
  235.5 7.3 %reduce-scatter.6.cloned.1.call-done = f32[128,1024]{1,0:T(8,128)} async-done(((f32[128,2048]{1,0:T(8,128)}), f32[128,1024]{1,0:T(8,128)}) %reduce-scatter.6.cloned.1.call-update) | async-done | bytes 524304 | tf_op jit(solution)/shard_map/reduce_scatter | solution.py:136
  242.8 1.2 multiply_reduce_fusion
  244.0 2.5 psum.15
  246.5 1.3 add_convert_fusion
  248.0 0.5 copy-done.8
  248.5 1.8 fusion.44
  250.3 0.4 fusion.45
  250.7 4.4 %fusion.19 = f32[8,512,128]{1,2,0:T(8,128)} fusion(bf16[128,8,128]{0,2,1:T(8,128)(2,1)} %bitcast.80, bf16[8,128,512]{2,1,0:T(8,128)(2,1)S(1)} %divide_convert_fusion, f32[8,128,512]{2,1,0:T(8,128)} %fusion.44), kind=kOutput, calls=%fused_computation.29 | convolution fusion | flops 137889280 | bytes 5505024 | tf_op jit(solution)/shard_map/hqk,qhd->khd/dot_general | solution.py:153
  255.1 2.9 copy.48
  258.0 1.8 copy.49
  259.8 4.7 %pad_maximum_fusion = f32[512,2048]{1,0:T(8,128)} fusion(f32[512,1024]{1,0:T(8,128)} %copy.49, f32[512,1024]{1,0:T(8,128)} %copy.48), kind=kLoop, calls=%fused_computation.3 | loop fusion | flops 1048576 | bytes 8388608 | tf_op jit(solution)/shard_map/concatenate | solution.py:160
  264.5 1.2 copy-done.5
  265.9 4.4 %convert_bitcast_fusion.1 = bf16[1,2048,1024]{2,1,0:T(8,128)(2,1)} fusion(bf16[288,2048]{1,0:T(8,128)(2,1)S(1)} %copy-done.5, bf16[288,1024]{1,0:T(8,128)(2,1)S(1)} %copy-done.16), kind=kOutput, calls=%fused_computation.15 | convolution fusion | flops 1210056704 | bytes 5963776 | tf_op jit(solution)/shard_map/dot_general | solution.py:115
  270.3 4.4 %convert_bitcast_fusion.2 = bf16[1,2048,1024]{2,1,0:T(8,128)(2,1)} fusion(bf16[288,2048]{1,0:T(8,128)(2,1)S(1)} %copy-done.5, bf16[288,1024]{1,0:T(8,128)(2,1)S(1)} %copy-done.22), kind=kOutput, calls=%fused_computation.16 | convolution fusion | flops 1210056704 | bytes 5963776 | tf_op jit(solution)/shard_map/dot_general | solution.py:112
  274.7 4.4 %convert_bitcast_fusion = bf16[1,1024,2048]{2,1,0:T(8,128)(2,1)} fusion(bf16[288,2048]{1,0:T(8,128)(2,1)S(1)} %copy-done.3, f32[288,1024]{1,0:T(8,128)S(1)} %copy-done.20, f32[288,1024]{1,0:T(8,128)S(1)} %copy-done.18), kind=kOutput, calls=%fused_computation.14 | convolution fusion | flops 1211826176 | bytes 7733248 | tf_op jit(solution)/shard_map/dot_general | solution.py:109
  279.1 3.0 fusion.21
  282.1 0.9 copy.50
  283.0 59.6 %reduce-scatter.8.cloned.1.call-done = f32[128,2048]{1,0:T(8,128)} async-done(((f32[512,2048]{1,0:T(8,128)}), f32[128,2048]{1,0:T(8,128)}) %reduce-scatter.8.cloned.1.call-update) | async-done | bytes 1048592 | tf_op jit(solution)/shard_map/reduce_scatter | solution.py:159
  342.6 1.3 convert.4
  343.9 0.8 fusion.42
  (63 shorter events, 1.5 us)
Async XLA Ops:
  7.2 6.9 %copy-start.10 = (s32[128,1]{0,1:T(1,128)S(1)}, s32[128,1]{0,1:T(1,128)}, u32[]{:S(2)}) copy-start(s32[128,1]{0,1:T(1,128)} %param.14) | copy-start | bytes 1540
  7.2 13.1 %copy-start.9 = (bf16[128,1024]{1,0:T(8,128)(2,1)S(1)}, bf16[128,1024]{1,0:T(8,128)(2,1)}, u32[]{:S(2)}) copy-start(bf16[128,1024]{1,0:T(8,128)(2,1)} %param.9) | copy-start | bytes 786436
  7.2 35.9 %all-gather.7.cloned.1.call-start = ((), (), s32[]{:S(2)}) async-start(), calls=%async_computation.6 | async-start | bytes 1310720 | tf_op jit(solution)/shard_map/all_gather | solution.py:47
  9.1 61.9 %all-gather.9.cloned.1.call-start = ((), (), s32[]{:S(2)}) async-start(), calls=%async_computation.7 | async-start | bytes 1310720 | tf_op jit(solution)/shard_map/all_gather | solution.py:48
  15.2 12.0 %all-to-all-start = ((bf16[4,18,2048]{2,1,0:T(8,128)(2,1)}), bf16[4,18,2048]{2,1,0:T(8,128)(2,1)S(1)}, u32[]{:S(2)}, u32[]{:S(2)}) async-start(bf16[4,18,2048]{2,1,0:T(8,128)(2,1)} %reshape.148), calls=%async_computation | async-start | bytes 786432 | tf_op jit(solution)/shard_map/all_to_all | solution.py:89
  20.2 89.5 %all-gather.11.cloned.1.call-start = ((), (), s32[]{:S(2)}) async-start(), calls=%async_computation.11 | async-start | bytes 1966080 | tf_op jit(solution)/shard_map/all_gather | solution.py:93
  20.4 52.0 %copy-start.6 = (bf16[128,1024]{0,1:T(8,128)(2,1)}, bf16[128,1024]{0,1:T(8,128)(2,1)S(1)}, u32[]{:S(2)}) copy-start(bf16[128,1024]{0,1:T(8,128)(2,1)S(1)} %copy.53) | copy-start | bytes 786436
  27.2 0.7 copy-start.1
  27.9 119.2 %all-gather.13.cloned.1.call-start = ((), (), s32[]{:S(2)}) async-start(), calls=%async_computation.12 | async-start | bytes 1966080 | tf_op jit(solution)/shard_map/all_gather | solution.py:92
  74.3 1.0 copy-start
  93.2 117.4 %reduce-scatter.4.cloned.1.call-start = ((), (), s32[]{:S(2)}) async-start(), calls=%async_computation.8 | async-start | bytes 2949120 | tf_op jit(solution)/shard_map/reduce_scatter | solution.py:119
  149.5 4.1 %copy-start.4 = (bf16[288,2048]{1,0:T(8,128)(2,1)S(1)}, bf16[288,2048]{1,0:T(8,128)(2,1)}, u32[]{:S(2)}) copy-start(bf16[288,2048]{1,0:T(8,128)(2,1)} %reshape.151) | copy-start | bytes 3538948
  149.5 4.1 %copy-start.13 = (bf16[1,2048,1024]{2,1,0:T(8,128)(2,1)S(1)}, bf16[1,2048,1024]{2,1,0:T(8,128)(2,1)}, u32[]{:S(2)}) copy-start(bf16[1,2048,1024]{2,1,0:T(8,128)(2,1)} %param.16) | copy-start | bytes 12582916
  153.7 1.4 copy-start.17
  153.7 1.7 copy-start.2
  153.7 3.0 copy-start.11
  156.6 1.8 copy-start.19
  156.6 2.6 copy-start.12
  158.4 2.3 copy-start.21
  158.4 2.3 copy-start.15
  212.6 15.2 %all-to-all-start.2 = ((f32[4,18,2048]{2,1,0:T(8,128)}), f32[4,18,2048]{2,1,0:T(8,128)}, u32[]{:S(2)}, u32[]{:S(2)}) async-start(f32[4,18,2048]{2,1,0:T(8,128)} %reshape.152), calls=%async_computation.3 | async-start | bytes 1572864 | tf_op jit(solution)/shard_map/all_to_all | solution.py:125
  216.8 26.0 %reduce-scatter.6.cloned.1.call-start = ((), (), s32[]{:S(2)}) async-start(), calls=%async_computation.9 | async-start | bytes 1572864 | tf_op jit(solution)/shard_map/reduce_scatter | solution.py:136
  232.9 13.6 %copy-start.7 = (bf16[128,1024]{1,0:T(8,128)(2,1)S(1)}, bf16[128,1024]{1,0:T(8,128)(2,1)}, u32[]{:S(2)}) copy-start(bf16[128,1024]{1,0:T(8,128)(2,1)} %param.13) | copy-start | bytes 786436
  235.3 107.3 %reduce-scatter.8.cloned.1.call-start = ((), (), s32[]{:S(2)}) async-start(), calls=%async_computation.10 | async-start | bytes 5242880 | tf_op jit(solution)/shard_map/reduce_scatter | solution.py:159
  247.8 0.7 copy-start.8
  264.5 1.3 copy-start.5
  264.5 1.4 copy-start.16
  265.9 4.4 %copy-start.22 = (bf16[288,1024]{1,0:T(8,128)(2,1)S(1)}, bf16[288,1024]{1,0:T(8,128)(2,1)}, u32[]{:S(2)}) copy-start(bf16[288,1024]{1,0:T(8,128)(2,1)} %copy-done.21) | copy-start | bytes 1769476
  270.3 4.4 %copy-start.3 = (bf16[288,2048]{1,0:T(8,128)(2,1)S(1)}, bf16[288,2048]{1,0:T(8,128)(2,1)}, u32[]{:S(2)}) copy-start(bf16[288,2048]{1,0:T(8,128)(2,1)} %reshape.149) | copy-start | bytes 3538948
  270.3 4.4 %copy-start.18 = (f32[288,1024]{1,0:T(8,128)S(1)}, f32[288,1024]{1,0:T(8,128)}, u32[]{:S(2)}) copy-start(f32[288,1024]{1,0:T(8,128)} %copy-done.17) | copy-start | bytes 3538948
  270.3 4.4 %copy-start.20 = (f32[288,1024]{1,0:T(8,128)S(1)}, f32[288,1024]{1,0:T(8,128)}, u32[]{:S(2)}) copy-start(f32[288,1024]{1,0:T(8,128)} %copy-done.19) | copy-start | bytes 3538948
  274.7 4.5 %copy-start.14 = (bf16[512,1024]{0,1:T(8,128)(2,1)S(1)}, bf16[512,1024]{0,1:T(8,128)(2,1)}, u32[]{:S(2)}) copy-start(bf16[512,1024]{0,1:T(8,128)(2,1)} %all-gather.7.cloned.1.call-done) | copy-start | bytes 3145732
Sparse Core Ops, SparseCore 0:
  10.2 32.9 all-gather.6
  44.7 26.2 all-gather.8
  73.1 36.5 all-gather.10
  111.1 35.9 all-gather.12
  163.7 46.8 reduce-scatter.3
  235.4 7.3 reduce-scatter.5
  264.6 77.9 reduce-scatter.7
where the time goes:
time: 353 us; the launch traced here: 352 us
  waiting for transfers between devices  223 us (63%)
  matrix products  39.4 us (11%)
  local copies, waits for them, and re-layouts  29.3 us (8%)
  blocking collectives  20.6 us (6%)
  other arithmetic  14.8 us (4%)
  between operations  14.4 us (4%)
  starting transfers between devices  9.71 us (3%)
    reduce_scatter x1, waiting for transfers between devices, on_device(): lax.psum_scatter(jnp.concatenate([key_part.reshape(lax.axis_size('context...  59.6 us
    reduce_scatter x1, waiting for transfers between devices, on_device(): lax.psum_scatter(term + jnp.einsum('rf,df->rd', grad_up_rows, up_local, p...  47 us
    all_gather x1, waiting for transfers between devices, on_device(): lax.all_gather(got_normed[None], 'context', axis=0, tiled=True)  35 us
    all_gather x1, waiting for transfers between devices, on_device(): lax.all_gather(value_input, 'context', axis=0, tiled=True)  24.4 us
    all_gather x1, waiting for transfers between devices, on_device(): lax.all_gather(got_grad[None], 'context', axis=0, tiled=True)  16.5 us
    all_gather x1, waiting for transfers between devices, on_device(): lax.all_gather(key_input, 'context', axis=0, tiled=True)  15.1 us
    all_to_all x1, blocking collectives, on_device(): lax.all_to_all(send_normed, 'expert', split_axis=0, concat_axis=0, tiled=...  11 us
    all_to_all x1, waiting for transfers between devices, on_device(): lax.all_to_all(summed_rows.reshape(n_expert, capacity, -1), 'expert', spl...  10.9 us
  transfers between devices with their start and end apart: 9, of which 9 were waited for; matrix products, arithmetic and copies ran while one was open for 9% of the time, Pallas kernels for 0%

commit v1 on v0

--- a/solution.py
+++ b/solution.py
@@ -1,9 +1,14 @@
+import functools
+
 import jax
 import jax.numpy as jnp
 from jax import lax
+from jax.experimental import pallas as pl
+from jax.experimental.pallas import tpu as pltpu
 from jax.sharding import PartitionSpec as P
 
 HD = 128
+MESH = pl.DeviceIdType.MESH
 
 
 EPSILON = 1e-06
@@ -174,9 +179,420 @@
     return (grad_queries, grad_keys, grad_values, grad_residual, grad_gate, grad_up, grad_down)
 
 
+def remote(src, dst, send_sem, recv_sem, target):
+    return pltpu.make_async_remote_copy(
+        src_ref=src,
+        dst_ref=dst,
+        send_sem=send_sem,
+        recv_sem=recv_sem,
+        device_id=target,
+        device_id_type=MESH,
+    )
+
+
+def position():
+    return lax.axis_index("expert"), lax.axis_index("context"), lax.axis_index("tensor")
+
+
+def partner(step, sizes):
+    n_expert, n_context, n_tensor = sizes
+    own_expert, own_context, own_tensor = position()
+    own = (own_expert * n_context + own_context) * n_tensor + own_tensor
+    other = lax.rem(own + step, n_expert * n_context * n_tensor)
+    return (
+        other // (n_context * n_tensor),
+        lax.rem(other // n_tensor, n_context),
+        lax.rem(other, n_tensor),
+    )
+
+
+def greet_all(sizes):
+    n_devices = sizes[0] * sizes[1] * sizes[2]
+    barrier = pltpu.get_barrier_semaphore()
+
+    @pl.loop(1, n_devices)
+    def _(step):
+        pl.semaphore_signal(barrier, inc=1, device_id=partner(step, sizes), device_id_type=MESH)
+
+    return barrier, n_devices - 1
+
+
+def aligned(start, size):
+    return pl.ds(pl.multiple_of(start, size), size)
+
+
+def dot(left, right, left_dim=1, right_dim=0):
+    return lax.dot_general(
+        left, right, (((left_dim,), (right_dim,)), ((), ())), preferred_element_type=jnp.float32
+    )
+
+
+def forward_kernel(sizes, rows, slots, ids_ref, q_ref, k_ref, v_ref, r_ref, g_ref,
+                   x_out, g_out, place_ref, probs_ref, qh, kh, vh, gh,
+                   rh, ids_all, state, x_send, g_send,
+                   in_send, in_recv, out_send, out_recv):
+    n_expert, n_context, n_tensor = sizes
+    n_devices = n_expert * n_context * n_tensor
+    n_all = n_expert * n_tensor
+    own_expert, own_context, own_tensor = position()
+    width = qh.shape[1]
+    length = qh.shape[0]
+    barrier, count = greet_all(sizes)
+    pl.semaphore_wait(barrier, count)
+    moves = [(g_ref, gh), (q_ref, qh), (k_ref, kh), (v_ref, vh), (r_ref, rh)]
+
+    def in_copy(number, step):
+        target = lax.rem(own_context + step, n_context)
+        if number == len(moves):
+            src, dst = ids_ref, ids_all.at[own_context]
+        else:
+            src = moves[number][0].at[:, aligned(target * width, width)]
+            dst = moves[number][1].at[aligned(own_context * rows, rows), :]
+        return remote(src, dst, in_send.at[number, step], in_recv.at[number, step],
+                      (own_expert, target, own_tensor))
+
+    for number in [len(moves), 0, 1, 2, 3, 4]:
+        for step in range(1, n_context):
+            in_copy(number, step).start()
+    ids_all[own_context] = ids_ref[...]
+    for src, dst in moves:
+        dst[aligned(own_context * rows, rows), :] = src[:, aligned(own_context * width, width)]
+
+    def arrived(number):
+        for step in range(1, n_context):
+            in_copy(number, step).wait_recv()
+
+    def out_copy(kind, step):
+        src, dst = ((g_send, g_out), (x_send, x_out))[kind]
+        expert, context, tensor = partner(step, sizes)
+        return remote(
+            src.at[aligned((expert * n_tensor + tensor) * slots, slots), :],
+            dst.at[aligned(own_expert * slots, slots),
+                   aligned((own_tensor * n_context + own_context) * width, width)],
+            out_send.at[kind, step], out_recv.at[kind, step], (expert, context, tensor))
+
+    def dispatch(kind, send, out, source):
+        for e in range(n_all):
+            send[e * slots:(e + 1) * slots, :] = dot(
+                place_ref[e * slots:(e + 1) * slots, :], source[...]).astype(jnp.bfloat16)
+
+        @pl.loop(1, n_devices)
+        def _(step):
+            out_copy(kind, step).start()
+
+        out[aligned(own_expert * slots, slots),
+            aligned((own_tensor * n_context + own_context) * width, width)] = send[
+                aligned((own_expert * n_tensor + own_tensor) * slots, slots), :]
+
+    arrived(len(moves))
+    named = lax.broadcasted_iota(jnp.int32, (n_all, rows), 0)
+    onehot = jnp.concatenate(
+        [(ids_all[c] == named).astype(jnp.float32) for c in range(n_context)], axis=1)
+    before = (lax.broadcasted_iota(jnp.int32, (length, length), 0)
+              < lax.broadcasted_iota(jnp.int32, (length, length), 1))
+    rank = dot(onehot.astype(jnp.bfloat16), before.astype(jnp.float32).astype(jnp.bfloat16))
+    rank = jnp.where(onehot > 0.5, rank, -1.0)
+    slot = lax.broadcasted_iota(jnp.int32, (slots, length), 0).astype(jnp.float32)
+    for e in range(n_all):
+        place_ref[e * slots:(e + 1) * slots, :] = (
+            (rank[e:e + 1, :] == slot).astype(jnp.float32).astype(jnp.bfloat16))
+    arrived(0)
+    dispatch(0, g_send, g_out, gh)
+    for number in (1, 2, 3, 4):
+        arrived(number)
+    heads = width // HD
+    for h in range(heads):
+        cols = slice(h * HD, (h + 1) * HD)
+        for c in range(n_context):
+            seen = (c + 1) * rows
+            block = slice(c * rows, seen)
+            scores = dot(qh[block, cols], kh[:seen, cols], 1, 1) * HD ** (-0.5)
+            query = c * rows + lax.broadcasted_iota(jnp.int32, (rows, seen), 0)
+            key = lax.broadcasted_iota(jnp.int32, (rows, seen), 1)
+            scores = jnp.where(key <= query, scores, -jnp.inf)
+            shifted = jnp.exp(scores - jnp.max(scores, axis=1, keepdims=True))
+            probs = (shifted / jnp.sum(shifted, axis=1, keepdims=True)).astype(jnp.bfloat16)
+            probs_ref[h, block, :seen] = probs
+            attn = dot(probs, vh[:seen, cols]).astype(jnp.bfloat16).astype(jnp.float32)
+            state[block, cols] = (rh[block, cols].astype(jnp.float32) + attn).astype(jnp.bfloat16)
+    dispatch(1, x_send, x_out, state)
+
+    @pl.loop(1, n_devices)
+    def _(step):
+        for kind in (0, 1):
+            out_copy(kind, step).wait()
+
+    for number in range(len(moves) + 1):
+        for step in range(1, n_context):
+            in_copy(number, step).wait_send()
+
+
+def expert_kernel(sizes, slots, tile, x_ref, g_ref, gate_hbm, up_hbm, down_hbm,
+                  back, grad_gate_hbm, grad_up_hbm, grad_down_hbm,
+                  gate_w, up_w, down_w, act, dgate, dup, inv_ref, inner_ref, r_send,
+                  gate_out, up_out, down_out, load_sem, store_sem, send_sem, recv_sem):
+    n_expert, n_context, n_tensor = sizes
+    n_devices = n_expert * n_context * n_tensor
+    n_all = n_expert * n_tensor
+    own_expert, own_context, own_tensor = position()
+    features, hidden = gate_w.shape
+    tiles = hidden // tile
+    width = r_send.shape[2]
+    pieces = features // width
+
+    def load(number, f):
+        part = aligned(f * tile, tile)
+        src, dst = ((gate_hbm.at[0, :, part], gate_w.at[:, part]),
+                    (up_hbm.at[0, :, part], up_w.at[:, part]),
+                    (down_hbm.at[0, part, :], down_w.at[part, :]))[number]
+        return pltpu.make_async_copy(src, dst, load_sem.at[number, f])
+
+    for f in range(tiles):
+        for number in range(3):
+            load(number, f).start()
+    barrier, count = greet_all(sizes)
+    x32 = x_ref[...].astype(jnp.float32)
+    inv_ref[...] = 1.0 / jnp.sqrt(
+        jnp.sum(x32 * x32, axis=1, keepdims=True) / features + EPSILON)
+    inner_ref[...] = jnp.zeros_like(inner_ref)
+    for f in range(tiles):
+        part = slice(f * tile, (f + 1) * tile)
+        for number in range(3):
+            load(number, f).wait()
+        inv = inv_ref[...]
+        gate = dot(x_ref[...], gate_w[:, part]) * inv
+        up = dot(x_ref[...], up_w[:, part]) * inv
+        grad_act = dot(g_ref[...], down_w[part, :], 1, 1)
+        sig = 1.0 / (1.0 + jnp.exp(-gate))
+        grad_up = grad_act * gate * sig
+        grad_gate = grad_act * up * sig * (1.0 + gate * (1.0 - sig))
+        act[:, part] = (gate * sig * up).astype(jnp.bfloat16)
+        inner_ref[...] += jnp.sum(grad_gate * gate + grad_up * up, axis=1, keepdims=True)
+        dgate[:, part] = (grad_gate * inv).astype(jnp.bfloat16)
+        dup[:, part] = (grad_up * inv).astype(jnp.bfloat16)
+    inner_ref[...] = inner_ref[...] * inv_ref[...] * inv_ref[...] / features
+    pl.semaphore_wait(barrier, count)
+
+    def piece_copy(piece, seq):
+        tensor, context = piece // n_context, lax.rem(piece, n_context)
+        return remote(
+            r_send.at[piece, aligned(seq * slots, slots), :],
+            back.at[own_context, aligned((own_expert * n_tensor + own_tensor) * slots, slots), :],
+            send_sem.at[piece, seq],
+            recv_sem.at[own_context, own_expert * n_tensor + own_tensor],
+            (seq, context, tensor))
+
+    def is_own(piece, seq):
+        return (piece == own_tensor * n_context + own_context) & (seq == own_expert)
+
+    @pl.loop(0, pieces)
+    def _(turn):
+        piece = lax.rem(own_tensor * n_context + own_context + 1 + turn, pieces)
+        part = aligned(piece * width, width)
+        grad = dot(dgate[...], gate_w[part, :], 1, 1) + dot(dup[...], up_w[part, :], 1, 1)
+        grad = grad - x_ref[:, part].astype(jnp.float32) * inner_ref[...]
+        r_send[piece] = grad.astype(jnp.bfloat16)
+
+        @pl.loop(0, n_expert)
+        def _(seq):
+            @pl.when(jnp.logical_not(is_own(piece, seq)))
+            def _():
+                piece_copy(piece, seq).start()
+
+    back[own_context, aligned((own_expert * n_tensor + own_tensor) * slots, slots), :] = r_send[
+        own_tensor * n_context + own_context, aligned(own_expert * slots, slots), :]
+
+    def store(number, f):
+        part = aligned(f * tile, tile)
+        src, dst = ((gate_out.at[:, part], grad_gate_hbm.at[0, :, part]),
+                    (up_out.at[:, part], grad_up_hbm.at[0, :, part]),
+                    (down_out.at[part, :], grad_down_hbm.at[0, part, :]))[number]
+        return pltpu.make_async_copy(src, dst, store_sem.at[number, f])
+
+    for f in range(tiles):
+        part = slice(f * tile, (f + 1) * tile)
+        down_out[part, :] = dot(act[:, part], g_ref[...], 0, 0).astype(jnp.bfloat16)
+        store(2, f).start()
+        gate_out[:, part] = dot(x_ref[...], dgate[:, part], 0, 0).astype(jnp.bfloat16)
+        store(0, f).start()
+        up_out[:, part] = dot(x_ref[...], dup[:, part], 0, 0).astype(jnp.bfloat16)
+        store(1, f).start()
+
+    @pl.loop(0, pieces)
+    def _(piece):
+        @pl.loop(0, n_expert)
+        def _(seq):
+            @pl.when(jnp.logical_not(is_own(piece, seq)))
+            def _():
+                piece_copy(piece, seq).wait_send()
+
+    @pl.loop(0, n_context)
+    def _(context):
+        @pl.loop(0, n_all)
+        def _(expert):
+            @pl.when(jnp.logical_not(
+                (context == own_context) & (expert == own_expert * n_tensor + own_tensor)))
+            def _():
+                part = back.at[context, aligned(expert * slots, slots), :]
+                pltpu.make_async_copy(part, part, recv_sem.at[context, expert]).wait()
+
+    for f in range(tiles):
+        for number in range(3):
+            store(number, f).wait()
+
+
+def backward_kernel(sizes, rows, back, place_ref, probs_ref, qh, kh, vh, gh,
+                    gq_out, gk_out, gv_out, gr_out,
+                    gq, gk, gv, gr, dk_sum, dv_sum, send_sem, recv_sem):
+    n_expert, n_context, n_tensor = sizes
+    own_expert, own_context, own_tensor = position()
+    width = qh.shape[1]
+    barrier = pltpu.get_barrier_semaphore()
+    for step in range(1, n_context):
+        pl.semaphore_signal(
+            barrier, inc=1,
+            device_id=(own_expert, lax.rem(own_context + step, n_context), own_tensor),
+            device_id_type=MESH)
+    moves = [(gr, gr_out), (gv, gv_out), (gk, gk_out), (gq, gq_out)]
+
+    def copy(number, step):
+        target = lax.rem(own_context + step, n_context)
+        src, dst = moves[number]
+        return remote(
+            src.at[aligned(target * rows, rows), :],
+            dst.at[:, aligned(own_context * width, width)],
+            send_sem.at[number, step], recv_sem.at[number, step],
+            (own_expert, target, own_tensor))
+
+    def send(number):
+        for step in range(1, n_context):
+            copy(number, step).start()
+        src, dst = moves[number]
+        dst[:, aligned(own_context * width, width)] = src[aligned(own_context * rows, rows), :]
+
+    change = dot(place_ref[...], back[0], 0, 0)
+    for context in range(1, n_context):
+        change = change + dot(place_ref[...], back[context], 0, 0)
+    gr[...] = (gh[...].astype(jnp.float32) + change).astype(jnp.bfloat16)
+    pl.semaphore_wait(barrier, n_context - 1)
+    send(0)
+    heads = width // HD
+    dk_sum[...] = jnp.zeros_like(dk_sum)
+    dv_sum[...] = jnp.zeros_like(dv_sum)
+    for h in range(heads):
+        cols = slice(h * HD, (h + 1) * HD)
+        for c in range(n_context):
+            seen = (c + 1) * rows
+            block = slice(c * rows, seen)
+            probs = probs_ref[h, block, :seen]
+            probs32 = probs.astype(jnp.float32)
+            grad_probs = dot(gr[block, cols], vh[:seen, cols], 1, 1)
+            row_dot = jnp.sum(probs32 * grad_probs, axis=1, keepdims=True)
+            grad_scores = (probs32 * (grad_probs - row_dot) * HD ** (-0.5)).astype(jnp.bfloat16)
+            gq[block, cols] = dot(grad_scores, kh[:seen, cols]).astype(jnp.bfloat16)
+            dk_sum[:seen, cols] += dot(grad_scores, qh[block, cols], 0, 0)
+            dv_sum[:seen, cols] += dot(probs, gr[block, cols], 0, 0)
+    gv[...] = dv_sum[...].astype(jnp.bfloat16)
+    send(1)
+    gk[...] = dk_sum[...].astype(jnp.bfloat16)
+    send(2)
+    send(3)
+    for number in range(len(moves)):
+        for step in range(1, n_context):
+            copy(number, step).wait()
+
+
+def by_heads(queries, key_input, value_input, residual, grad_output, expert_of,
+             gate_weight, up_weight, down_weight):
+    rows, local = queries.shape
+    n_expert, n_context, n_tensor = (
+        lax.axis_size("expert"), lax.axis_size("context"), lax.axis_size("tensor"))
+    sizes = (n_expert, n_context, n_tensor)
+    n_devices = n_expert * n_context * n_tensor
+    n_all = n_expert * n_tensor
+    features = local * n_tensor
+    width = local // n_context
+    length = rows * n_context
+    hidden = gate_weight.shape[2]
+    capacity = (rows // n_all + max(1, rows // (8 * n_all))) * n_context
+    slots = -(-capacity // 16) * 16
+    routed = n_expert * slots
+    bf16, f32 = jnp.bfloat16, jnp.float32
+    vmem = pl.BlockSpec(memory_space=pltpu.VMEM)
+    hbm = pl.BlockSpec(memory_space=pl.ANY)
+    dma = pltpu.SemaphoreType.DMA
+    ids = jnp.broadcast_to(expert_of.reshape(1, rows), (n_all, rows))
+
+    def shape(*dims):
+        return jax.ShapeDtypeStruct(dims, bf16)
+
+    x_rows, g_rows, place, probs, qh, kh, vh, gh = pl.pallas_call(
+        functools.partial(forward_kernel, sizes, rows, slots),
+        out_shape=[shape(routed, features), shape(routed, features),
+                   shape(n_all * slots, length), shape(width // HD, length, length)]
+        + [shape(length, width)] * 4,
+        in_specs=[vmem] * 6,
+        out_specs=[vmem] * 8,
+        scratch_shapes=[
+            pltpu.VMEM((length, width), bf16),
+            pltpu.VMEM((n_context, n_all, rows), jnp.int32),
+            pltpu.VMEM((length, width), bf16),
+            pltpu.VMEM((n_all * slots, width), bf16),
+            pltpu.VMEM((n_all * slots, width), bf16),
+            dma((6, n_context)), dma((6, n_context)), dma((2, n_devices)), dma((2, n_devices)),
+        ],
+        compiler_params=pltpu.CompilerParams(
+            collective_id=0, has_side_effects=True, vmem_limit_bytes=48 << 20),
+    )(ids, queries, key_input, value_input, residual, grad_output)
+    tile = min(hidden, 256)
+    back, grad_gate, grad_up, grad_down = pl.pallas_call(
+        functools.partial(expert_kernel, sizes, slots, tile),
+        out_shape=[shape(n_context, n_all * slots, width), shape(*gate_weight.shape),
+                   shape(*up_weight.shape), shape(*down_weight.shape)],
+        in_specs=[vmem, vmem, hbm, hbm, hbm],
+        out_specs=[vmem, hbm, hbm, hbm],
+        scratch_shapes=[
+            pltpu.VMEM((features, hidden), bf16),
+            pltpu.VMEM((features, hidden), bf16),
+            pltpu.VMEM((hidden, features), bf16),
+            pltpu.VMEM((routed, hidden), bf16),
+            pltpu.VMEM((routed, hidden), bf16),
+            pltpu.VMEM((routed, hidden), bf16),
+            pltpu.VMEM((routed, 1), f32),
+            pltpu.VMEM((routed, 1), f32),
+            pltpu.VMEM((features // width, routed, width), bf16),
+            pltpu.VMEM((features, hidden), bf16),
+            pltpu.VMEM((features, hidden), bf16),
+            pltpu.VMEM((hidden, features), bf16),
+            dma((3, hidden // tile)), dma((3, hidden // tile)),
+            dma((features // width, n_expert)), dma((n_context, n_all)),
+        ],
+        compiler_params=pltpu.CompilerParams(
+            collective_id=1, has_side_effects=True, vmem_limit_bytes=56 << 20),
+    )(x_rows, g_rows, gate_weight, up_weight, down_weight)
+    grad_queries, grad_keys, grad_values, grad_residual = pl.pallas_call(
+        functools.partial(backward_kernel, sizes, rows),
+        out_shape=[shape(rows, local)] * 4,
+        in_specs=[vmem] * 7,
+        out_specs=[vmem] * 4,
+        scratch_shapes=[pltpu.VMEM((length, width), bf16)] * 4
+        + [pltpu.VMEM((length, width), f32)] * 2
+        + [dma((4, n_context)), dma((4, n_context))],
+        compiler_params=pltpu.CompilerParams(
+            collective_id=2, has_side_effects=True, vmem_limit_bytes=48 << 20),
+    )(back, place, probs, qh, kh, vh, gh)
+    return (grad_queries, grad_keys, grad_values, grad_residual, grad_gate, grad_up, grad_down)
+
+
+def on_one(queries, *rest):
+    if (queries.shape[1] // HD) % lax.axis_size("context") == 0:
+        return by_heads(queries, *rest)
+    return on_device(queries, *rest)
+
+
 def solution(mesh):
     return jax.shard_map(
-        on_device,
+        on_one,
         mesh=mesh,
         in_specs=(
             P(("expert", "context"), "tensor"),

time: 353 us -> 184 us (0.52)
  waiting for transfers between devices: 223 us -> 0 us
  Pallas kernels: 0 us -> 163 us
  matrix products: 39.4 us -> 0 us
  blocking collectives: 20.6 us -> 0 us
  other arithmetic: 14.8 us -> 0 us
  between operations: 14.4 us -> 0.69 us
  starting transfers between devices: 9.71 us -> 0 us
  local copies, waits for them, and re-layouts: 29.3 us -> 20 us
    pallas_call x0 -> x3, Pallas kernels: none -> 163 us  [the longest x1 94 us: by_heads(): pl.pallas_call(functools.partial(forward_kernel, sizes, rows, slots), out...]
    reduce_scatter x3 -> x0, waiting for transfers between devices: 114 us -> none  [the longest x1 59.6 us: on_device(): lax.psum_scatter(jnp.concatenate([key_part.reshape(lax.axis_size('context...]
    all_gather x4 -> x0, waiting for transfers between devices: 91.1 us -> none  [the longest x1 35 us: on_device(): lax.all_gather(got_normed[None], 'context', axis=0, tiled=True)]
    dot_general x15 -> x0, matrix products: 36 us -> none  [the longest x1 4.44 us: on_device(): jnp.dot(activation.T, routed_grad, preferred_element_type=jnp.float32)]
    all_to_all x2 -> x0, waiting for transfers between devices: 17.5 us -> none  [the longest x1 10.9 us: on_device(): lax.all_to_all(summed_rows.reshape(n_expert, capacity, -1), 'expert', spl...]
    reshape x10 -> x0, local copies, waits for them, and re-layouts: 15.7 us -> none  [the longest x1 2.88 us: on_device(): key_part.reshape(lax.axis_size('context') * row_count, -1)]
    unnamed x48 -> x27, local copies, waits for them, and re-layouts: 8.17 us -> 19.3 us
    all_to_all x1 -> x0, blocking collectives: 11 us -> none  [on_device(): lax.all_to_all(send_normed, 'expert', split_axis=0, concat_axis=0, tiled=...]
  transfers between devices with their start and end apart: 9 -> 0, of which waited for: 9 -> 0; matrix products, arithmetic and copies ran while one was open for 9% -> 0% of each run, Pallas kernels for 0% -> 0%
where the time goes in v1:
time: 184 us; the launch traced here: 183 us
  Pallas kernels  163 us (89%)
  local copies, waits for them, and re-layouts  20 us (11%)
    pallas_call x1, Pallas kernels, by_heads(): pl.pallas_call(functools.partial(forward_kernel, sizes, rows, slots), out...  94 us
    pallas_call x1, Pallas kernels, by_heads(): pl.pallas_call(functools.partial(expert_kernel, sizes, slots, tile), out_...  40.1 us
    pallas_call x1, Pallas kernels, by_heads(): pl.pallas_call(functools.partial(backward_kernel, sizes, rows), out_shape...  28.5 us
    unnamed x27, local copies, waits for them, and re-layouts  19.3 us

profile of v1, /device:TPU:0, one launch (start us, length us, event | category | flops | bytes accessed | tf_op | source)
XLA Modules:
  0.0 183.2 jit_solution(2157369957626566945)
XLA Ops:
  0.6 0.7 broadcast_in_dim.8.ids_ref
  1.3 0.0 copy-start.2
  1.3 0.9 copy-done.2
  2.2 0.0 copy-start.3
  2.2 0.9 copy-done.3
  3.2 0.0 copy-start.4
  3.2 0.9 copy-done.4
  4.1 0.0 copy-start.5
  4.1 0.9 copy-done.5
  5.1 0.0 copy-start.6
  5.1 0.9 copy-done.6
  6.0 94.0 %shard_map.144 = (bf16[320,2048]{1,0:T(8,128)(2,1)S(1)}, bf16[320,2048]{1,0:T(8,128)(2,1)}, bf16[640,512]{1,0:T(8,128)(2,1)S(1)}, bf16[2,512,512]{2,1,0:T(8,128)...) custom-call(s32[8,128]{1,0:T(8,128)S(1)} %broadcast_in_dim.8.ids_ref, ...), custom_call_target="tpu_custom_call" | custom-call | tf_op jit(solution)/shard_map/pallas_call | solution.py:529
  100.0 0.0 copy-start.1
  100.0 1.0 copy-done.1
  101.1 40.1 %shard_map.145 = (bf16[4,640,256]{2,1,0:T(8,128)(2,1)}, bf16[1,2048,1024]{2,1,0:T(8,128)(2,1)}, bf16[1,2048,1024]{2,1,0:T(8,128)(2,1)}, bf16[1,1024,2048]{2,1,0:T(8,128)(2,1)}) custom-call(bf16[320,2048]{1,0:T(8,128)(2,1)} %copy-done.1, bf16[320,2048]{1,0:T(8,128)(2,1)} %get-tuple-element.24.g_ref, bf16[1,2048,1024]{2,1,0:T(8,128)(2,1)} %gate_hbm.1, ...), custom_call_target="tpu_custom_call" | custom-call | tf_op jit(solution)/shard_map/pallas_call | solution.py:548
  141.2 0.0 copy-start
  141.2 1.3 copy-done
  142.5 0.0 copy-start.9
  142.5 28.5 %shard_map.146 = (bf16[128,1024]{1,0:T(8,128)(2,1)S(1)}, bf16[128,1024]{1,0:T(8,128)(2,1)S(1)}, bf16[128,1024]{1,0:T(8,128)(2,1)S(1)}, bf16[128,1024]{1,0:T(8,128)(2,1)S(1)}) custom-call(bf16[4,640,256]{2,1,0:T(8,128)(2,1)S(1)} %copy-done, bf16[640,512]{1,0:T(8,128)(2,1)S(1)} %get-tuple-element.26.place_ref, ...), custom_call_target="tpu_custom_call" | custom-call | tf_op jit(solution)/shard_map/pallas_call | solution.py:573
  171.0 0.7 copy.23
  171.7 0.7 copy.24
  172.4 0.7 copy.25
  173.1 0.7 copy.26
  173.8 0.0 copy-done.9
  173.8 0.0 copy-start.8
  173.8 2.1 %copy.27 = bf16[1,2048,1024]{2,1,0:T(8,128)(2,1)} copy(bf16[1,2048,1024]{2,1,0:T(8,128)(2,1)S(1)} %copy-done.9) | data formatting | bytes 8388608
  175.9 1.6 copy-done.8
  177.5 0.0 copy-start.7
  177.5 2.1 %copy.28 = bf16[1,2048,1024]{2,1,0:T(8,128)(2,1)} copy(bf16[1,2048,1024]{2,1,0:T(8,128)(2,1)S(1)} %copy-done.8) | data formatting | bytes 8388608
  179.6 1.6 copy-done.7
  181.2 2.0 %copy.29 = bf16[1,1024,2048]{2,1,0:T(8,128)(2,1)} copy(bf16[1,1024,2048]{2,1,0:T(8,128)(2,1)S(1)} %copy-done.7) | data formatting | bytes 8388608
Async XLA Ops:
  1.3 0.9 copy-start.2
  2.2 0.9 copy-start.3
  3.2 0.9 copy-start.4
  4.1 0.9 copy-start.5
  5.1 0.9 copy-start.6
  100.0 1.1 copy-start.1
  141.2 1.3 copy-start
  142.5 31.3 %copy-start.9 = (bf16[1,2048,1024]{2,1,0:T(8,128)(2,1)S(1)}, bf16[1,2048,1024]{2,1,0:T(8,128)(2,1)}, u32[]{:S(2)}) copy-start(bf16[1,2048,1024]{2,1,0:T(8,128)(2,1)} %get-tuple-element.50) | copy-start | bytes 12582916
  173.8 3.7 %copy-start.8 = (bf16[1,2048,1024]{2,1,0:T(8,128)(2,1)S(1)}, bf16[1,2048,1024]{2,1,0:T(8,128)(2,1)}, u32[]{:S(2)}) copy-start(bf16[1,2048,1024]{2,1,0:T(8,128)(2,1)} %get-tuple-element.51) | copy-start | bytes 12582916
  177.5 3.7 %copy-start.7 = (bf16[1,1024,2048]{2,1,0:T(8,128)(2,1)S(1)}, bf16[1,1024,2048]{2,1,0:T(8,128)(2,1)}, u32[]{:S(2)}) copy-start(bf16[1,1024,2048]{2,1,0:T(8,128)(2,1)} %get-tuple-element.52) | copy-start | bytes 12582916

commit v2 on v0

--- a/solution.py
+++ b/solution.py
@@ -1,9 +1,14 @@
+import functools
+
 import jax
 import jax.numpy as jnp
 from jax import lax
+from jax.experimental import pallas as pl
+from jax.experimental.pallas import tpu as pltpu
 from jax.sharding import PartitionSpec as P
 
 HD = 128
+MESH = pl.DeviceIdType.MESH
 
 
 EPSILON = 1e-06
@@ -174,9 +179,536 @@
     return (grad_queries, grad_keys, grad_values, grad_residual, grad_gate, grad_up, grad_down)
 
 
+def remote(src, dst, send_sem, recv_sem, target):
+    return pltpu.make_async_remote_copy(
+        src_ref=src,
+        dst_ref=dst,
+        send_sem=send_sem,
+        recv_sem=recv_sem,
+        device_id=target,
+        device_id_type=MESH,
+    )
+
+
+def position():
+    return lax.axis_index("expert"), lax.axis_index("context"), lax.axis_index("tensor")
+
+
+def greet_all(sizes):
+    n_expert, n_context, n_tensor = sizes
+    n_devices = n_expert * n_context * n_tensor
+    own_expert, own_context, own_tensor = position()
+    own = (own_expert * n_context + own_context) * n_tensor + own_tensor
+    barrier = pltpu.get_barrier_semaphore()
+
+    @pl.loop(1, n_devices)
+    def _(step):
+        other = lax.rem(own + step, n_devices)
+        target = (
+            other // (n_context * n_tensor),
+            lax.rem(other // n_tensor, n_context),
+            lax.rem(other, n_tensor),
+        )
+        pl.semaphore_signal(barrier, inc=1, device_id=target, device_id_type=MESH)
+
+    return barrier, n_devices - 1
+
+
+def aligned(start, size):
+    return pl.ds(pl.multiple_of(start, size), size)
+
+
+def dot(left, right, left_dim=1, right_dim=0):
+    return lax.dot_general(
+        left, right, (((left_dim,), (right_dim,)), ((), ())), preferred_element_type=jnp.float32
+    )
+
+
+def as_bf16(mask):
+    return mask.astype(jnp.float32).astype(jnp.bfloat16)
+
+
+def layer_kernel(sizes, rows, capacity, slots, tile,
+                 ids_ref, q_ref, k_ref, v_ref, r_ref, g_ref, gate_hbm, up_hbm, down_hbm,
+                 gq_out, gk_out, gv_out, gr_out, down_hbm_out, x_turned, dgate, dup,
+                 qh, kh, vh, rh, gh, ids_all, place_ref, probs_ref, state,
+                 x_send, g_send, x_rows, g_land, g_rows,
+                 gate_w, up_w, down_w, act, grad_act_ref, inv_ref, inner_ref, r_send, back,
+                 down_out, gq, gk, gv, gr, dk_sum, dv_sum,
+                 own_sem, in_send, in_recv, plane_send, chain_send, land_recv,
+                 load_sem, store_sem, back_send, back_recv, out_send, out_recv):
+    n_expert, n_context, n_tensor = sizes
+    n_all = n_expert * n_tensor
+    own_expert, own_context, own_tensor = position()
+    own_piece = own_expert * n_tensor + own_tensor
+    length, width = qh.shape
+    heads = width // HD
+    features, hidden = gate_w.shape
+    tiles = hidden // tile
+    pieces = features // width
+    barrier, count = greet_all(sizes)
+
+    def load(number, f):
+        part = slice(f * tile, (f + 1) * tile)
+        src, dst = ((gate_hbm.at[0, :, part], gate_w.at[:, part]),
+                    (up_hbm.at[0, :, part], up_w.at[:, part]),
+                    (down_hbm.at[0, part, :], down_w.at[part, :]))[number]
+        return pltpu.make_async_copy(src, dst, load_sem.at[number, f])
+
+    moves = [(q_ref, qh), (k_ref, kh), (v_ref, vh), (r_ref, rh), (g_ref, gh)]
+    n_moves = len(moves)
+
+    def own_copy(number):
+        src, dst = moves[number]
+        return pltpu.make_async_copy(
+            src.at[:, aligned(own_context * width, width)],
+            dst.at[aligned(own_context * rows, rows), :], own_sem.at[number])
+
+    for number in range(n_moves):
+        own_copy(number).start()
+    ids_all[own_context] = ids_ref[...]
+
+    def in_copy(number, step):
+        target = lax.rem(own_context + step, n_context)
+        if number == n_moves:
+            src, dst = ids_ref, ids_all.at[own_context]
+        else:
+            src = moves[number][0].at[:, aligned(target * width, width)]
+            dst = moves[number][1].at[aligned(own_context * rows, rows), :]
+        return remote(src, dst, in_send.at[number, step], in_recv.at[number, step],
+                      (own_expert, target, own_tensor))
+
+    def start_in(number):
+        for step in range(1, n_context):
+            in_copy(number, step).start()
+
+    def arrived(number):
+        for step in range(1, n_context):
+            in_copy(number, step).wait_recv()
+        if number < n_moves:
+            own_copy(number).wait()
+
+    def land(kind, plane, piece):
+        if kind == 0:
+            return g_land.at[piece, plane]
+        seq, tensor = piece // n_tensor, lax.rem(piece, n_tensor)
+        return x_rows.at[aligned(seq * slots, slots),
+                         aligned((tensor * n_context + plane) * width, width)]
+
+    def plane_copy(kind, step):
+        other = lax.rem(own_piece + step, n_all)
+        src = (g_send, x_send)[kind]
+        return remote(
+            src.at[aligned(other * slots, slots), :], land(kind, own_context, own_piece),
+            plane_send.at[kind, step], land_recv.at[kind, own_context, own_piece],
+            (other // n_tensor, own_context, lax.rem(other, n_tensor)))
+
+    def chain_copy(kind, plane, piece, side):
+        part = land(kind, plane, piece)
+        return remote(
+            part, part, chain_send.at[kind, side, plane, piece], land_recv.at[kind, plane, piece],
+            (own_expert, own_context + (1, -1)[side], own_tensor))
+
+    def await_land(kind, plane, piece):
+        part = land(kind, plane, piece)
+        pltpu.make_async_copy(part, part, land_recv.at[kind, plane, piece]).wait()
+
+    has = (own_context < n_context - 1, own_context > 0)
+
+    def start_plane(kind):
+        @pl.loop(1, n_all)
+        def _(step):
+            plane_copy(kind, step).start()
+
+        src = (g_send, x_send)[kind]
+        mine = src[aligned(own_piece * slots, slots), :]
+        if kind == 0:
+            g_land[own_piece, own_context] = mine
+        else:
+            x_rows[aligned(own_expert * slots, slots),
+                   aligned((own_tensor * n_context + own_context) * width, width)] = mine
+
+    def pass_on(kind, away):
+        if away == 0:
+            @pl.loop(0, n_all)
+            def _(turn):
+                piece = lax.rem(own_piece + turn, n_all)
+
+                @pl.when(piece != own_piece)
+                def _():
+                    await_land(kind, own_context, piece)
+
+                for side in (0, 1):
+                    @pl.when(has[side])
+                    def _():
+                        chain_copy(kind, own_context, piece, side).start()
+            return
+        for side in (0, 1):
+            plane = own_context + (-away, away)[side]
+
+            @pl.when((plane >= 0) & (plane < n_context))
+            def _():
+                @pl.loop(0, n_all)
+                def _(piece):
+                    await_land(kind, plane, piece)
+
+                    @pl.when(has[side])
+                    def _():
+                        chain_copy(kind, plane, piece, side).start()
+
+    def chain_sent(kind):
+        @pl.loop(1, n_all)
+        def _(step):
+            plane_copy(kind, step).wait_send()
+
+        for away in range(n_context - 1):
+            for side in (0, 1):
+                plane = own_context + (-away, away)[side]
+
+                @pl.when((plane >= 0) & (plane < n_context) & has[side])
+                def _():
+                    @pl.loop(0, n_all)
+                    def _(piece):
+                        chain_copy(kind, plane, piece, side).wait_send()
+
+    named = lax.broadcasted_iota(jnp.int32, (n_all, rows), 0)
+    before = as_bf16(lax.broadcasted_iota(jnp.int32, (rows, rows), 0)
+                     < lax.broadcasted_iota(jnp.int32, (rows, rows), 1))
+    slot = lax.broadcasted_iota(jnp.int32, (slots, rows), 0).astype(jnp.float32)
+
+    def ranks(ids):
+        onehot = (ids == named).astype(jnp.float32)
+        return jnp.where(onehot > 0.5, dot(onehot.astype(jnp.bfloat16), before), -2.0 * slots)
+
+    own_rank = ranks(ids_ref[...])
+    pl.semaphore_wait(barrier, count)
+    for number in (n_moves, 0, 1, 2, 3):
+        start_in(number)
+    for f in range(tiles):
+        for number in (2, 0, 1):
+            load(number, f).start()
+    for e in range(n_all):
+        packed = jnp.zeros((slots, width), jnp.float32)
+        for j in range(n_context):
+            place = as_bf16(own_rank[e:e + 1, :] + j * capacity == slot)
+            packed = packed + dot(place, g_ref[:, j * width:(j + 1) * width])
+        g_send[e * slots:(e + 1) * slots, :] = packed.astype(jnp.bfloat16)
+    start_plane(0)
+    arrived(n_moves)
+    for c in range(n_context):
+        rank = ranks(ids_all[c])
+        for e in range(n_all):
+            place_ref[e * slots:(e + 1) * slots, c * rows:(c + 1) * rows] = as_bf16(
+                rank[e:e + 1, :] + c * capacity == slot)
+    pass_on(0, 0)
+    for number in range(4):
+        arrived(number)
+    for h in range(heads):
+        cols = slice(h * HD, (h + 1) * HD)
+        for c in range(n_context):
+            seen = (c + 1) * rows
+            block = slice(c * rows, seen)
+            scores = dot(qh[block, cols], kh[:seen, cols], 1, 1) * HD ** (-0.5)
+            query = c * rows + lax.broadcasted_iota(jnp.int32, (rows, seen), 0)
+            key = lax.broadcasted_iota(jnp.int32, (rows, seen), 1)
+            scores = jnp.where(key <= query, scores, -jnp.inf)
+            shifted = jnp.exp(scores - jnp.max(scores, axis=1, keepdims=True))
+            probs = (shifted / jnp.sum(shifted, axis=1, keepdims=True)).astype(jnp.bfloat16)
+            probs_ref[h, block, :seen] = probs
+            attn = dot(probs, vh[:seen, cols]).astype(jnp.bfloat16).astype(jnp.float32)
+            state[block, cols] = (rh[block, cols].astype(jnp.float32) + attn).astype(jnp.bfloat16)
+        if h == 0:
+            pass_on(0, 1)
+    for e in range(n_all):
+        x_send[e * slots:(e + 1) * slots, :] = dot(
+            place_ref[e * slots:(e + 1) * slots, :], state[...]).astype(jnp.bfloat16)
+    start_plane(1)
+    for away in range(2, n_context):
+        pass_on(0, away)
+        if away == 2:
+            pass_on(1, 0)
+    if n_context == 2:
+        pass_on(1, 0)
+    pass_on(1, 1)
+
+    out_row = lax.broadcasted_iota(jnp.int32, (slots, n_context * slots), 0)
+    in_row = lax.broadcasted_iota(jnp.int32, (slots, n_context * slots), 1)
+    unpack = []
+    for j in range(n_context):
+        match = jnp.zeros((slots, n_context * slots), jnp.float32)
+        for c in range(n_context):
+            match = match + (
+                (in_row == out_row + c * (slots - capacity) + j * capacity)
+                & (out_row >= c * capacity) & (out_row < (c + 1) * capacity)).astype(jnp.float32)
+        unpack.append(match)
+    unpack = jnp.concatenate(unpack, axis=0).astype(jnp.bfloat16)
+    for seq in range(n_expert):
+        for t in range(n_tensor):
+            landed = g_land[seq * n_tensor + t].reshape(n_context * slots, width)
+            parts = dot(unpack, landed).astype(jnp.bfloat16)
+            for j in range(n_context):
+                at = (t * n_context + j) * width
+                g_rows[seq * slots:(seq + 1) * slots, at:at + width] = parts[
+                    j * slots:(j + 1) * slots]
+    for away in range(2, n_context):
+        pass_on(1, away)
+        if away == 2:
+            start_in(4)
+    if n_context == 2:
+        start_in(4)
+    for f in range(tiles):
+        part = slice(f * tile, (f + 1) * tile)
+        for number in range(3):
+            load(number, f).wait()
+        grad_act_ref[:, part] = dot(g_rows[...], down_w[part, :], 1, 1)
+
+    x32 = x_rows[...].astype(jnp.float32)
+    inv_ref[...] = 1.0 / jnp.sqrt(
+        jnp.sum(x32 * x32, axis=1, keepdims=True) / features + EPSILON)
+    inner_ref[...] = jnp.zeros_like(inner_ref)
+    for f in range(tiles):
+        part = slice(f * tile, (f + 1) * tile)
+        inv = inv_ref[...]
+        gate = dot(x_rows[...], gate_w[:, part]) * inv
+        up = dot(x_rows[...], up_w[:, part]) * inv
+        grad_act = grad_act_ref[:, part]
+        sig = 1.0 / (1.0 + jnp.exp(-gate))
+        grad_up = grad_act * gate * sig
+        grad_gate = grad_act * up * sig * (1.0 + gate * (1.0 - sig))
+        act[:, part] = (gate * sig * up).astype(jnp.bfloat16)
+        inner_ref[...] += jnp.sum(grad_gate * gate + grad_up * up, axis=1, keepdims=True)
+        dgate[:, part] = (grad_gate * inv).astype(jnp.bfloat16)
+        dup[:, part] = (grad_up * inv).astype(jnp.bfloat16)
+    inner_ref[...] = inner_ref[...] * inv_ref[...] * inv_ref[...] / features
+
+    def piece_copy(piece, seq):
+        tensor, context = piece // n_context, lax.rem(piece, n_context)
+        return remote(
+            r_send.at[piece, aligned(seq * slots, slots), :],
+            back.at[own_context, aligned(own_piece * slots, slots), :],
+            back_send.at[piece, seq], back_recv.at[own_context, own_piece],
+            (seq, context, tensor))
+
+    def is_own(piece, seq):
+        return (piece == own_tensor * n_context + own_context) & (seq == own_expert)
+
+    @pl.loop(0, pieces)
+    def _(turn):
+        piece = lax.rem(own_tensor * n_context + own_context + 1 + turn, pieces)
+        part = aligned(piece * width, width)
+        grad = dot(dgate[...], gate_w[part, :], 1, 1) + dot(dup[...], up_w[part, :], 1, 1)
+        grad = grad - x_rows[:, part].astype(jnp.float32) * inner_ref[...]
+        r_send[piece] = grad.astype(jnp.bfloat16)
+
+        @pl.loop(0, n_expert)
+        def _(seq):
+            @pl.when(jnp.logical_not(is_own(piece, seq)))
+            def _():
+                piece_copy(piece, seq).start()
+
+    back[own_context, aligned(own_piece * slots, slots), :] = r_send[
+        own_tensor * n_context + own_context, aligned(own_expert * slots, slots), :]
+
+    def store(f):
+        part = slice(f * tile, (f + 1) * tile)
+        return pltpu.make_async_copy(
+            down_out.at[part, :], down_hbm_out.at[0, part, :], store_sem.at[f])
+
+    for f in range(tiles):
+        part = slice(f * tile, (f + 1) * tile)
+        down_out[part, :] = dot(act[:, part], g_rows[...], 0, 0).astype(jnp.bfloat16)
+        store(f).start()
+    x_turned[...] = x_rows[...].T
+    chain_sent(0)
+    chain_sent(1)
+    arrived(4)
+    for number in range(n_moves + 1):
+        for step in range(1, n_context):
+            in_copy(number, step).wait_send()
+
+    @pl.loop(0, n_context)
+    def _(context):
+        @pl.loop(0, n_all)
+        def _(piece):
+            @pl.when(jnp.logical_not((context == own_context) & (piece == own_piece)))
+            def _():
+                part = back.at[context, aligned(piece * slots, slots), :]
+                pltpu.make_async_copy(part, part, back_recv.at[context, piece]).wait()
+
+    outs = [(gr, gr_out), (gv, gv_out), (gk, gk_out), (gq, gq_out)]
+
+    def out_copy(number, step):
+        target = lax.rem(own_context + step, n_context)
+        src, dst = outs[number]
+        return remote(
+            src.at[aligned(target * rows, rows), :],
+            dst.at[:, aligned(own_context * width, width)],
+            out_send.at[number, step], out_recv.at[number, step],
+            (own_expert, target, own_tensor))
+
+    def send(number):
+        for step in range(1, n_context):
+            out_copy(number, step).start()
+        src, dst = outs[number]
+        dst[:, aligned(own_context * width, width)] = src[aligned(own_context * rows, rows), :]
+
+    change = dot(place_ref[...], back[0], 0, 0)
+    for context in range(1, n_context):
+        change = change + dot(place_ref[...], back[context], 0, 0)
+    gr[...] = (gh[...].astype(jnp.float32) + change).astype(jnp.bfloat16)
+    send(0)
+    dk_sum[...] = jnp.zeros_like(dk_sum)
+    dv_sum[...] = jnp.zeros_like(dv_sum)
+    for h in range(heads):
+        cols = slice(h * HD, (h + 1) * HD)
+        for c in range(n_context):
+            seen = (c + 1) * rows
+            block = slice(c * rows, seen)
+            dv_sum[:seen, cols] += dot(probs_ref[h, block, :seen], gr[block, cols], 0, 0)
+    gv[...] = dv_sum[...].astype(jnp.bfloat16)
+    send(1)
+    for h in range(heads):
+        cols = slice(h * HD, (h + 1) * HD)
+        for c in range(n_context):
+            seen = (c + 1) * rows
+            block = slice(c * rows, seen)
+            probs = probs_ref[h, block, :seen].astype(jnp.float32)
+            grad_probs = dot(gr[block, cols], vh[:seen, cols], 1, 1)
+            row_dot = jnp.sum(probs * grad_probs, axis=1, keepdims=True)
+            grad_scores = (probs * (grad_probs - row_dot) * HD ** (-0.5)).astype(jnp.bfloat16)
+            gq[block, cols] = dot(grad_scores, kh[:seen, cols]).astype(jnp.bfloat16)
+            dk_sum[:seen, cols] += dot(grad_scores, qh[block, cols], 0, 0)
+    gk[...] = dk_sum[...].astype(jnp.bfloat16)
+    send(2)
+    send(3)
+
+    @pl.loop(0, pieces)
+    def _(piece):
+        @pl.loop(0, n_expert)
+        def _(seq):
+            @pl.when(jnp.logical_not(is_own(piece, seq)))
+            def _():
+                piece_copy(piece, seq).wait_send()
+
+    for f in range(tiles):
+        store(f).wait()
+    for number in range(len(outs)):
+        for step in range(1, n_context):
+            out_copy(number, step).wait()
+
+
+def finish_kernel(tile, x_turned, dgate, dup, *refs):
+    given, written = refs[:5], refs[5:10]
+    grad_gate_hbm, grad_up_hbm, gate_out, up_out, copy_sem, store_sem = refs[10:]
+    copies = [pltpu.make_async_copy(src, dst, copy_sem.at[i])
+              for i, (src, dst) in enumerate(zip(given, written))]
+    for copy in copies:
+        copy.start()
+    stores = []
+    for f in range(dgate.shape[1] // tile):
+        part = slice(f * tile, (f + 1) * tile)
+        for number, (rows_ref, out, hbm) in enumerate(
+                ((dgate, gate_out, grad_gate_hbm), (dup, up_out, grad_up_hbm))):
+            out[:, part] = dot(x_turned[...], rows_ref[:, part]).astype(jnp.bfloat16)
+            stores.append(pltpu.make_async_copy(
+                out.at[:, part], hbm.at[0, :, part], store_sem.at[number, f]))
+            stores[-1].start()
+    for copy in copies + stores:
+        copy.wait()
+
+
+def by_heads(queries, key_input, value_input, residual, grad_output, expert_of,
+             gate_weight, up_weight, down_weight):
+    rows, local = queries.shape
+    n_expert, n_context, n_tensor = (
+        lax.axis_size("expert"), lax.axis_size("context"), lax.axis_size("tensor"))
+    sizes = (n_expert, n_context, n_tensor)
+    n_all = n_expert * n_tensor
+    features = local * n_tensor
+    width = local // n_context
+    length = rows * n_context
+    hidden = gate_weight.shape[2]
+    capacity = rows // n_all + max(1, rows // (8 * n_all))
+    slots = -(-capacity * n_context // 16) * 16
+    routed = n_expert * slots
+    tile = min(hidden, 256)
+    tiles = hidden // tile
+    bf16, f32 = jnp.bfloat16, jnp.float32
+    vmem = pl.BlockSpec(memory_space=pltpu.VMEM)
+    hbm = pl.BlockSpec(memory_space=pl.ANY)
+    dma = pltpu.SemaphoreType.DMA
+    ids = jnp.broadcast_to(expert_of.reshape(1, rows), (n_all, rows))
+
+    def shape(*dims):
+        return jax.ShapeDtypeStruct(dims, bf16)
+
+    def scratch(*dims, dtype=bf16):
+        return pltpu.VMEM(dims, dtype)
+
+    by_head = scratch(length, width)
+    *small, down_grad, x_turned, dgate, dup = pl.pallas_call(
+        functools.partial(layer_kernel, sizes, rows, capacity, slots, tile),
+        out_shape=[shape(rows, local)] * 4
+        + [shape(*down_weight.shape), shape(features, routed),
+           shape(routed, hidden), shape(routed, hidden)],
+        in_specs=[vmem, hbm, hbm, hbm, hbm, vmem, hbm, hbm, hbm],
+        out_specs=[vmem] * 4 + [hbm] + [vmem] * 3,
+        scratch_shapes=[
+            by_head, by_head, by_head, by_head, by_head,
+            scratch(n_context, n_all, rows, dtype=jnp.int32),
+            scratch(n_all * slots, length),
+            scratch(width // HD, length, length),
+            by_head,
+            scratch(n_all * slots, width),
+            scratch(n_all * slots, width),
+            scratch(routed, features),
+            scratch(n_all, n_context, slots, width),
+            scratch(routed, features),
+            scratch(features, hidden),
+            scratch(features, hidden),
+            scratch(hidden, features),
+            scratch(routed, hidden),
+            scratch(routed, hidden, dtype=f32),
+            scratch(routed, 1, dtype=f32),
+            scratch(routed, 1, dtype=f32),
+            scratch(features // width, routed, width),
+            scratch(n_context, n_all * slots, width),
+            scratch(hidden, features),
+            by_head, by_head, by_head, by_head,
+            scratch(length, width, dtype=f32),
+            scratch(length, width, dtype=f32),
+            dma((5,)), dma((6, n_context)), dma((6, n_context)),
+            dma((2, n_all)), dma((2, 2, n_context, n_all)), dma((2, n_context, n_all)),
+            dma((3, tiles)), dma((tiles,)),
+            dma((features // width, n_expert)), dma((n_context, n_all)),
+            dma((4, n_context)), dma((4, n_context)),
+        ],
+        compiler_params=pltpu.CompilerParams(
+            collective_id=0, has_side_effects=True, vmem_limit_bytes=52 << 20),
+    )(ids, queries, key_input, value_input, residual, grad_output,
+      gate_weight, up_weight, down_weight)
+    *small, down_grad, gate_grad, up_grad = pl.pallas_call(
+        functools.partial(finish_kernel, tile),
+        out_shape=[shape(rows, local)] * 4
+        + [shape(*down_weight.shape), shape(*gate_weight.shape), shape(*up_weight.shape)],
+        in_specs=[vmem] * 3 + [hbm] * 5,
+        out_specs=[hbm] * 7,
+        scratch_shapes=[
+            scratch(features, hidden), scratch(features, hidden), dma((5,)), dma((2, tiles))],
+        compiler_params=pltpu.CompilerParams(vmem_limit_bytes=24 << 20),
+    )(x_turned, dgate, dup, *small, down_grad)
+    return (*small, gate_grad, up_grad, down_grad)
+
+
+def on_one(queries, *rest):
+    if (queries.shape[1] // HD) % lax.axis_size("context") == 0:
+        return by_heads(queries, *rest)
+    return on_device(queries, *rest)
+
+
 def solution(mesh):
     return jax.shard_map(
-        on_device,
+        on_one,
         mesh=mesh,
         in_specs=(
             P(("expert", "context"), "tensor"),

time: 353 us -> 156 us (0.44)
  waiting for transfers between devices: 223 us -> 0 us
  Pallas kernels: 0 us -> 144 us
  matrix products: 39.4 us -> 0 us
  blocking collectives: 20.6 us -> 0 us
  local copies, waits for them, and re-layouts: 29.3 us -> 9.27 us
  other arithmetic: 14.8 us -> 0 us
  between operations: 14.4 us -> 0.82 us
  starting transfers between devices: 9.71 us -> 0 us
    pallas_call x0 -> x2, Pallas kernels: none -> 144 us  [the longest x1 137 us: by_heads(): pl.pallas_call(functools.partial(layer_kernel, sizes, rows, capacity, slo...]
    reduce_scatter x3 -> x0, waiting for transfers between devices: 114 us -> none  [the longest x1 59.6 us: on_device(): lax.psum_scatter(jnp.concatenate([key_part.reshape(lax.axis_size('context...]
    all_gather x4 -> x0, waiting for transfers between devices: 91.1 us -> none  [the longest x1 35 us: on_device(): lax.all_gather(got_normed[None], 'context', axis=0, tiled=True)]
    dot_general x15 -> x0, matrix products: 36 us -> none  [the longest x1 4.44 us: on_device(): jnp.dot(activation.T, routed_grad, preferred_element_type=jnp.float32)]
    all_to_all x2 -> x0, waiting for transfers between devices: 17.5 us -> none  [the longest x1 10.9 us: on_device(): lax.all_to_all(summed_rows.reshape(n_expert, capacity, -1), 'expert', spl...]
    reshape x10 -> x0, local copies, waits for them, and re-layouts: 15.7 us -> none  [the longest x1 2.88 us: on_device(): key_part.reshape(lax.axis_size('context') * row_count, -1)]
    all_to_all x1 -> x0, blocking collectives: 11 us -> none  [on_device(): lax.all_to_all(send_normed, 'expert', split_axis=0, concat_axis=0, tiled=...]
    all_to_all x2 -> x0, starting transfers between devices: 9.28 us -> none  [the longest x1 5.08 us: on_device(): lax.all_to_all(send_grad, 'expert', split_axis=0, concat_axis=0, tiled=True)]
  transfers between devices with their start and end apart: 9 -> 0, of which waited for: 9 -> 0; matrix products, arithmetic and copies ran while one was open for 9% -> 0% of each run, Pallas kernels for 0% -> 0%
where the time goes in v2:
time: 156 us; the launch traced here: 154 us
  Pallas kernels  144 us (92%)
  local copies, waits for them, and re-layouts  9.27 us (6%)
    pallas_call x1, Pallas kernels, by_heads(): pl.pallas_call(functools.partial(layer_kernel, sizes, rows, capacity, slo...  137 us
    unnamed x14, local copies, waits for them, and re-layouts  8.61 us
    pallas_call x1, Pallas kernels, by_heads(): pl.pallas_call(functools.partial(finish_kernel, tile), out_shape=[shape(r...  7.47 us

profile of v2, /device:TPU:0, one launch (start us, length us, event | category | flops | bytes accessed | tf_op | source)
XLA Modules:
  0.0 154.2 jit_solution(10946359193651905494)
XLA Ops:
  0.6 0.7 broadcast_in_dim.8.ids_ref
  1.3 0.0 copy-start.4
  1.3 0.9 copy-done.4
  2.2 0.0 copy-start.5
  2.2 0.9 copy-done.5
  3.2 0.0 copy-start.6
  3.2 0.9 copy-done.6
  4.1 136.6 %shard_map.144 = (bf16[128,1024]{1,0:T(8,128)(2,1)S(1)}, bf16[128,1024]{1,0:T(8,128)(2,1)S(1)}, bf16[128,1024]{1,0:T(8,128)(2,1)S(1)}, bf16[128,1024]{1,0:T(8,12...) custom-call(s32[8,128]{1,0:T(8,128)S(1)} %broadcast_in_dim.8.ids_ref, ...), custom_call_target="tpu_custom_call" | custom-call | tf_op jit(solution)/shard_map/pallas_call | solution.py:649
  140.8 0.0 copy-start
  140.8 2.2 %copy-done = bf16[1,1024,2048]{2,1,0:T(8,128)(2,1)S(1)} copy-done((bf16[1,1024,2048]{2,1,0:T(8,128)(2,1)S(1)}, bf16[1,1024,2048]{2,1,0:T(8,128)(2,1)}, u32[]{:S(2)}) %copy-start) | copy-done | bytes 4194328
  143.0 0.0 copy-start.1
  143.0 1.4 copy-done.1
  144.4 0.0 copy-start.2
  144.4 1.1 copy-done.2
  145.5 0.0 copy-start.3
  145.5 1.1 copy-done.3
  146.5 7.5 %shard_map.145 = (bf16[128,1024]{1,0:T(8,128)(2,1)}, bf16[128,1024]{1,0:T(8,128)(2,1)}, bf16[128,1024]{1,0:T(8,128)(2,1)}, bf16[128,1024]{1,0:T(8,128)(2,1)}, bf...) custom-call(bf16[2048,320]{1,0:T(8,128)(2,1)S(1)} %copy-done.1, ...), custom_call_target="tpu_custom_call" | custom-call | tf_op jit(solution)/shard_map/pallas_call | solution.py:690
Async XLA Ops:
  1.3 0.9 copy-start.4
  2.2 0.9 copy-start.5
  3.2 0.9 copy-start.6
  140.8 2.2 %copy-start = (bf16[1,1024,2048]{2,1,0:T(8,128)(2,1)S(1)}, bf16[1,1024,2048]{2,1,0:T(8,128)(2,1)}, u32[]{:S(2)}) copy-start(bf16[1,1024,2048]{2,1,0:T(8,128)(2,1)} %get-tuple-element.29.refs_4_) | copy-start | bytes 12582916
  143.0 1.4 copy-start.1
  144.4 1.1 copy-start.2
  145.5 1.1 copy-start.3

commit v3 on v2

--- a/solution.py
+++ b/solution.py
@@ -179,6 +179,9 @@
     return (grad_queries, grad_keys, grad_values, grad_residual, grad_gate, grad_up, grad_down)
 
 
+LANES = 128
+
+
 def remote(src, dst, send_sem, recv_sem, target):
     return pltpu.make_async_remote_copy(
         src_ref=src,
@@ -228,15 +231,27 @@
     return mask.astype(jnp.float32).astype(jnp.bfloat16)
 
 
+def pack(ref, at, value, rows):
+    for b in range(value.shape[1] // LANES):
+        ref[(*at, slice(b * rows, (b + 1) * rows), slice(None))] = value[
+            :, b * LANES:(b + 1) * LANES]
+
+
+def unpacked(ref, at, rows, width):
+    return jnp.concatenate(
+        [ref[(*at, slice(b * rows, (b + 1) * rows), slice(None))]
+         for b in range(width // LANES)], axis=1)
+
+
 def layer_kernel(sizes, rows, capacity, slots, tile,
                  ids_ref, q_ref, k_ref, v_ref, r_ref, g_ref, gate_hbm, up_hbm, down_hbm,
                  gq_out, gk_out, gv_out, gr_out, down_hbm_out, x_turned, dgate, dup,
                  qh, kh, vh, rh, gh, ids_all, place_ref, probs_ref, state,
-                 x_send, g_send, x_rows, g_land, g_rows,
-                 gate_w, up_w, down_w, act, grad_act_ref, inv_ref, inner_ref, r_send, back,
+                 x_send, g_send, x_land, g_land, x_rows, g_rows,
+                 gate_w, up_w, down_w, act, grad_act_ref, inv_ref, inner_ref, r_send, back, pair_land,
                  down_out, gq, gk, gv, gr, dk_sum, dv_sum,
                  own_sem, in_send, in_recv, plane_send, chain_send, land_recv,
-                 load_sem, store_sem, back_send, back_recv, out_send, out_recv):
+                 load_sem, store_sem, back_send, back_recv, pair_send, pair_recv, out_send, out_recv):
     n_expert, n_context, n_tensor = sizes
     n_all = n_expert * n_tensor
     own_expert, own_context, own_tensor = position()
@@ -289,17 +304,13 @@
             own_copy(number).wait()
 
     def land(kind, plane, piece):
-        if kind == 0:
-            return g_land.at[piece, plane]
-        seq, tensor = piece // n_tensor, lax.rem(piece, n_tensor)
-        return x_rows.at[aligned(seq * slots, slots),
-                         aligned((tensor * n_context + plane) * width, width)]
+        return (g_land, x_land)[kind].at[piece, plane]
 
     def plane_copy(kind, step):
         other = lax.rem(own_piece + step, n_all)
         src = (g_send, x_send)[kind]
         return remote(
-            src.at[aligned(other * slots, slots), :], land(kind, own_context, own_piece),
+            src.at[other], land(kind, own_context, own_piece),
             plane_send.at[kind, step], land_recv.at[kind, own_context, own_piece],
             (other // n_tensor, own_context, lax.rem(other, n_tensor)))
 
@@ -320,13 +331,7 @@
         def _(step):
             plane_copy(kind, step).start()
 
-        src = (g_send, x_send)[kind]
-        mine = src[aligned(own_piece * slots, slots), :]
-        if kind == 0:
-            g_land[own_piece, own_context] = mine
-        else:
-            x_rows[aligned(own_expert * slots, slots),
-                   aligned((own_tensor * n_context + own_context) * width, width)] = mine
+        (g_land, x_land)[kind][own_piece, own_context] = (g_send, x_send)[kind][own_piece]
 
     def pass_on(kind, away):
         if away == 0:
@@ -392,7 +397,7 @@
         for j in range(n_context):
             place = as_bf16(own_rank[e:e + 1, :] + j * capacity == slot)
             packed = packed + dot(place, g_ref[:, j * width:(j + 1) * width])
-        g_send[e * slots:(e + 1) * slots, :] = packed.astype(jnp.bfloat16)
+        pack(g_send, (e,), packed.astype(jnp.bfloat16), slots)
     start_plane(0)
     arrived(n_moves)
     for c in range(n_context):
@@ -420,16 +425,15 @@
         if h == 0:
             pass_on(0, 1)
     for e in range(n_all):
-        x_send[e * slots:(e + 1) * slots, :] = dot(
-            place_ref[e * slots:(e + 1) * slots, :], state[...]).astype(jnp.bfloat16)
+        pack(x_send, (e,), dot(
+            place_ref[e * slots:(e + 1) * slots, :], state[...]).astype(jnp.bfloat16), slots)
     start_plane(1)
-    for away in range(2, n_context):
+    pass_on(1, 0)
+    if n_context > 2:
+        pass_on(0, 2)
+    pass_on(1, 1)
+    for away in range(3, n_context):
         pass_on(0, away)
-        if away == 2:
-            pass_on(1, 0)
-    if n_context == 2:
-        pass_on(1, 0)
-    pass_on(1, 1)
 
     out_row = lax.broadcasted_iota(jnp.int32, (slots, n_context * slots), 0)
     in_row = lax.broadcasted_iota(jnp.int32, (slots, n_context * slots), 1)
@@ -444,7 +448,9 @@
     unpack = jnp.concatenate(unpack, axis=0).astype(jnp.bfloat16)
     for seq in range(n_expert):
         for t in range(n_tensor):
-            landed = g_land[seq * n_tensor + t].reshape(n_context * slots, width)
+            landed = jnp.concatenate(
+                [unpacked(g_land, (seq * n_tensor + t, c), slots, width)
+                 for c in range(n_context)], axis=0)
             parts = dot(unpack, landed).astype(jnp.bfloat16)
             for j in range(n_context):
                 at = (t * n_context + j) * width
@@ -462,6 +468,12 @@
             load(number, f).wait()
         grad_act_ref[:, part] = dot(g_rows[...], down_w[part, :], 1, 1)
 
+    for seq in range(n_expert):
+        for t in range(n_tensor):
+            for c in range(n_context):
+                at = (t * n_context + c) * width
+                x_rows[seq * slots:(seq + 1) * slots, at:at + width] = unpacked(
+                    x_land, (seq * n_tensor + t, c), slots, width)
     x32 = x_rows[...].astype(jnp.float32)
     inv_ref[...] = 1.0 / jnp.sqrt(
         jnp.sum(x32 * x32, axis=1, keepdims=True) / features + EPSILON)
@@ -481,33 +493,82 @@
         dup[:, part] = (grad_up * inv).astype(jnp.bfloat16)
     inner_ref[...] = inner_ref[...] * inv_ref[...] * inv_ref[...] / features
 
-    def piece_copy(piece, seq):
-        tensor, context = piece // n_context, lax.rem(piece, n_context)
+    paired = n_context == 4
+    half, low = own_context // 2, lax.rem(own_context, 2)
+    is_end = lax.rem(half + low + 1, 2)
+    per_half = pieces // 2
+
+    def piece_of(turn):
+        if not paired:
+            return turn // n_context, lax.rem(turn, n_context), False
+        first = 1 - turn // per_half
+        across = lax.rem(is_end + first + 1, 2)
+        k = lax.rem(turn, per_half)
+        context = lax.rem(half + across, 2) * 2 + lax.rem(k, 2)
+        return k // 2, context, across == 1
+
+    def piece_copy(tensor, context, seq):
+        piece = tensor * n_context + context
         return remote(
-            r_send.at[piece, aligned(seq * slots, slots), :],
-            back.at[own_context, aligned(own_piece * slots, slots), :],
+            r_send.at[piece, seq], back.at[own_context, own_piece],
             back_send.at[piece, seq], back_recv.at[own_context, own_piece],
             (seq, context, tensor))
 
-    def is_own(piece, seq):
-        return (piece == own_tensor * n_context + own_context) & (seq == own_expert)
+    def pair_copy(tensor, context):
+        k = tensor * 2 + lax.rem(context, 2)
+        return remote(
+            r_send.at[tensor * n_context + context], pair_land.at[k],
+            pair_send.at[k], pair_recv.at[k],
+            (own_expert, own_context + 1 - 2 * half, own_tensor))
+
+    def each_seq(tensor, context, act_on):
+        @pl.loop(0, n_expert)
+        def _(seq):
+            @pl.when(jnp.logical_not(
+                (context == own_context) & (tensor == own_tensor) & (seq == own_expert)))
+            def _():
+                act_on(piece_copy(tensor, context, seq))
 
     @pl.loop(0, pieces)
     def _(turn):
-        piece = lax.rem(own_tensor * n_context + own_context + 1 + turn, pieces)
+        tensor, context, across = piece_of(turn)
+        piece = tensor * n_context + context
         part = aligned(piece * width, width)
         grad = dot(dgate[...], gate_w[part, :], 1, 1) + dot(dup[...], up_w[part, :], 1, 1)
         grad = grad - x_rows[:, part].astype(jnp.float32) * inner_ref[...]
-        r_send[piece] = grad.astype(jnp.bfloat16)
-
-        @pl.loop(0, n_expert)
-        def _(seq):
-            @pl.when(jnp.logical_not(is_own(piece, seq)))
-            def _():
-                piece_copy(piece, seq).start()
-
-    back[own_context, aligned(own_piece * slots, slots), :] = r_send[
-        own_tensor * n_context + own_context, aligned(own_expert * slots, slots), :]
+        if not paired:
+            for seq in range(n_expert):
+                pack(r_send, (piece, seq),
+                     grad[seq * slots:(seq + 1) * slots].astype(jnp.bfloat16), slots)
+            each_seq(tensor, context, lambda copy: copy.start())
+            return
+        gather = across & (is_end == 0)
+
+        @pl.when(jnp.logical_not(gather))
+        def _():
+            for seq in range(n_expert):
+                pack(r_send, (piece, seq),
+                     grad[seq * slots:(seq + 1) * slots].astype(jnp.bfloat16), slots)
+
+        @pl.when(gather)
+        def _():
+            k = tensor * 2 + lax.rem(context, 2)
+            part = pair_land.at[k]
+            pltpu.make_async_copy(part, part, pair_recv.at[k]).wait()
+            for seq in range(n_expert):
+                both = grad[seq * slots:(seq + 1) * slots] + unpacked(
+                    pair_land, (k, seq), slots, width).astype(jnp.float32)
+                pack(r_send, (piece, seq), both.astype(jnp.bfloat16), slots)
+
+        @pl.when(across & (is_end == 1))
+        def _():
+            pair_copy(tensor, context).start()
+
+        @pl.when(jnp.logical_not(across & (is_end == 1)))
+        def _():
+            each_seq(tensor, context, lambda copy: copy.start())
+
+    back[own_context, own_piece] = r_send[own_tensor * n_context + own_context, own_expert]
 
     def store(f):
         part = slice(f * tile, (f + 1) * tile)
@@ -526,14 +587,7 @@
         for step in range(1, n_context):
             in_copy(number, step).wait_send()
 
-    @pl.loop(0, n_context)
-    def _(context):
-        @pl.loop(0, n_all)
-        def _(piece):
-            @pl.when(jnp.logical_not((context == own_context) & (piece == own_piece)))
-            def _():
-                part = back.at[context, aligned(piece * slots, slots), :]
-                pltpu.make_async_copy(part, part, back_recv.at[context, piece]).wait()
+    sources = [half * 2, half * 2 + 1, 2 - half] if paired else list(range(n_context))
 
     outs = [(gr, gr_out), (gv, gv_out), (gk, gk_out), (gq, gq_out)]
 
@@ -552,9 +606,18 @@
         src, dst = outs[number]
         dst[:, aligned(own_context * width, width)] = src[aligned(own_context * rows, rows), :]
 
-    change = dot(place_ref[...], back[0], 0, 0)
-    for context in range(1, n_context):
-        change = change + dot(place_ref[...], back[context], 0, 0)
+    change = jnp.zeros((length, width), jnp.float32)
+    for source in sources:
+        @pl.loop(0, n_all)
+        def _(piece):
+            @pl.when(jnp.logical_not((source == own_context) & (piece == own_piece)))
+            def _():
+                part = back.at[source, piece]
+                pltpu.make_async_copy(part, part, back_recv.at[source, piece]).wait()
+
+        landed = jnp.concatenate(
+            [unpacked(back, (source, piece), slots, width) for piece in range(n_all)], axis=0)
+        change = change + dot(place_ref[...], landed, 0, 0)
     gr[...] = (gh[...].astype(jnp.float32) + change).astype(jnp.bfloat16)
     send(0)
     dk_sum[...] = jnp.zeros_like(dk_sum)
@@ -583,12 +646,19 @@
     send(3)
 
     @pl.loop(0, pieces)
-    def _(piece):
-        @pl.loop(0, n_expert)
-        def _(seq):
-            @pl.when(jnp.logical_not(is_own(piece, seq)))
-            def _():
-                piece_copy(piece, seq).wait_send()
+    def _(turn):
+        tensor, context, across = piece_of(turn)
+        if not paired:
+            each_seq(tensor, context, lambda copy: copy.wait_send())
+            return
+
+        @pl.when(across & (is_end == 1))
+        def _():
+            pair_copy(tensor, context).wait_send()
+
+        @pl.when(jnp.logical_not(across & (is_end == 1)))
+        def _():
+            each_seq(tensor, context, lambda copy: copy.wait_send())
 
     for f in range(tiles):
         store(f).wait()
@@ -597,13 +667,18 @@
             out_copy(number, step).wait()
 
 
-def finish_kernel(tile, x_turned, dgate, dup, *refs):
+def finish_kernel(tile, x_hbm, dgate_hbm, dup_hbm, *refs):
     given, written = refs[:5], refs[5:10]
-    grad_gate_hbm, grad_up_hbm, gate_out, up_out, copy_sem, store_sem = refs[10:]
+    grad_gate_hbm, grad_up_hbm, x_turned, dgate, dup, gate_out, up_out = refs[10:17]
+    load_sem, copy_sem, store_sem = refs[17:]
+    loads = [pltpu.make_async_copy(src, dst, load_sem.at[i]) for i, (src, dst) in enumerate(
+        ((x_hbm, x_turned), (dgate_hbm, dgate), (dup_hbm, dup)))]
     copies = [pltpu.make_async_copy(src, dst, copy_sem.at[i])
               for i, (src, dst) in enumerate(zip(given, written))]
-    for copy in copies:
+    for copy in loads + copies:
         copy.start()
+    for copy in loads:
+        copy.wait()
     stores = []
     for f in range(dgate.shape[1] // tile):
         part = slice(f * tile, (f + 1) * tile)
@@ -629,7 +704,8 @@
     length = rows * n_context
     hidden = gate_weight.shape[2]
     capacity = rows // n_all + max(1, rows // (8 * n_all))
-    slots = -(-capacity * n_context // 16) * 16
+    slots = capacity * n_context
+    piece_rows = -(-slots * (width // LANES) // 16) * 16
     routed = n_expert * slots
     tile = min(hidden, 256)
     tiles = hidden // tile
@@ -659,10 +735,11 @@
             scratch(n_all * slots, length),
             scratch(width // HD, length, length),
             by_head,
-            scratch(n_all * slots, width),
-            scratch(n_all * slots, width),
+            scratch(n_all, piece_rows, LANES),
+            scratch(n_all, piece_rows, LANES),
+            scratch(n_all, n_context, piece_rows, LANES),
+            scratch(n_all, n_context, piece_rows, LANES),
             scratch(routed, features),
-            scratch(n_all, n_context, slots, width),
             scratch(routed, features),
             scratch(features, hidden),
             scratch(features, hidden),
@@ -671,8 +748,9 @@
             scratch(routed, hidden, dtype=f32),
             scratch(routed, 1, dtype=f32),
             scratch(routed, 1, dtype=f32),
-            scratch(features // width, routed, width),
-            scratch(n_context, n_all * slots, width),
+            scratch(features // width, n_expert, piece_rows, LANES),
+            scratch(n_context, n_all, piece_rows, LANES),
+            scratch(2 * n_tensor, n_expert, piece_rows, LANES),
             scratch(hidden, features),
             by_head, by_head, by_head, by_head,
             scratch(length, width, dtype=f32),
@@ -681,21 +759,24 @@
             dma((2, n_all)), dma((2, 2, n_context, n_all)), dma((2, n_context, n_all)),
             dma((3, tiles)), dma((tiles,)),
             dma((features // width, n_expert)), dma((n_context, n_all)),
+            dma((2 * n_tensor,)), dma((2 * n_tensor,)),
             dma((4, n_context)), dma((4, n_context)),
         ],
         compiler_params=pltpu.CompilerParams(
-            collective_id=0, has_side_effects=True, vmem_limit_bytes=52 << 20),
+            collective_id=0, has_side_effects=True, vmem_limit_bytes=60 << 20),
     )(ids, queries, key_input, value_input, residual, grad_output,
       gate_weight, up_weight, down_weight)
     *small, down_grad, gate_grad, up_grad = pl.pallas_call(
         functools.partial(finish_kernel, tile),
         out_shape=[shape(rows, local)] * 4
         + [shape(*down_weight.shape), shape(*gate_weight.shape), shape(*up_weight.shape)],
-        in_specs=[vmem] * 3 + [hbm] * 5,
+        in_specs=[hbm] * 8,
         out_specs=[hbm] * 7,
         scratch_shapes=[
-            scratch(features, hidden), scratch(features, hidden), dma((5,)), dma((2, tiles))],
-        compiler_params=pltpu.CompilerParams(vmem_limit_bytes=24 << 20),
+            scratch(features, routed), scratch(routed, hidden), scratch(routed, hidden),
+            scratch(features, hidden), scratch(features, hidden),
+            dma((3,)), dma((5,)), dma((2, tiles))],
+        compiler_params=pltpu.CompilerParams(vmem_limit_bytes=60 << 20),
     )(x_turned, dgate, dup, *small, down_grad)
     return (*small, gate_grad, up_grad, down_grad)
 

time: 156 us -> 291 us (1.87)
  Pallas kernels: 144 us -> 289 us
  local copies, waits for them, and re-layouts: 9.27 us -> 1.25 us
    pallas_call x1, Pallas kernels: 7.47 us -> 160 us  [by_heads(): pl.pallas_call(functools.partial(finish_kernel, tile), out_shape=[shape(r...]
    unnamed x14 -> x0, local copies, waits for them, and re-layouts: 8.61 us -> none
    pallas_call x1, Pallas kernels: 137 us -> 129 us  [by_heads(): pl.pallas_call(functools.partial(layer_kernel, sizes, rows, capacity, slo...]
where the time goes in v3:
time: 291 us
  Pallas kernels  289 us (99%)
    pallas_call x1, Pallas kernels, by_heads(): pl.pallas_call(functools.partial(finish_kernel, tile), out_shape=[shape(r...  160 us
    pallas_call x1, Pallas kernels, by_heads(): pl.pallas_call(functools.partial(layer_kernel, sizes, rows, capacity, slo...  129 us

profile of v3, /device:TPU:0, one launch (start us, length us, event | category | flops | bytes accessed | tf_op | source)
XLA Modules:
  0.0 290.8 jit_solution(7238960845795061840)
XLA Ops:
  0.6 1.2 broadcast_in_dim.8.ids_ref
  1.9 128.6 %shard_map.144 = (bf16[128,1024]{1,0:T(8,128)(2,1)}, bf16[128,1024]{1,0:T(8,128)(2,1)}, bf16[128,1024]{1,0:T(8,128)(2,1)}, bf16[128,1024]{1,0:T(8,128)(2,1)}, bf...) custom-call(s32[8,128]{1,0:T(8,128)} %broadcast_in_dim.8.ids_ref, ...), custom_call_target="tpu_custom_call" | custom-call | tf_op jit(solution)/shard_map/pallas_call | solution.py:725
  130.5 160.1 %shard_map.145 = (bf16[128,1024]{1,0:T(8,128)(2,1)}, bf16[128,1024]{1,0:T(8,128)(2,1)}, bf16[128,1024]{1,0:T(8,128)(2,1)}, bf16[128,1024]{1,0:T(8,128)(2,1)}, bf...) custom-call(bf16[2048,288]{1,0:T(8,128)(2,1)} %get-tuple-element.22.x_hbm, ...), custom_call_target="tpu_custom_call" | custom-call | tf_op jit(solution)/shard_map/pallas_call | solution.py:769

commit v4 on v3

--- a/solution.py
+++ b/solution.py
@@ -248,7 +248,7 @@
                  gq_out, gk_out, gv_out, gr_out, down_hbm_out, x_turned, dgate, dup,
                  qh, kh, vh, rh, gh, ids_all, place_ref, probs_ref, state,
                  x_send, g_send, x_land, g_land, x_rows, g_rows,
-                 gate_w, up_w, down_w, act, grad_act_ref, inv_ref, inner_ref, r_send, back, pair_land,
+                 gate_w, up_w, down_w, act, grad_act_ref, gate_sum, up_sum, inv_ref, inner_ref, r_send, back, pair_land,
                  down_out, gq, gk, gv, gr, dk_sum, dv_sum,
                  own_sem, in_send, in_recv, plane_send, chain_send, land_recv,
                  load_sem, store_sem, back_send, back_recv, pair_send, pair_recv, out_send, out_recv):
@@ -456,33 +456,53 @@
                 at = (t * n_context + j) * width
                 g_rows[seq * slots:(seq + 1) * slots, at:at + width] = parts[
                     j * slots:(j + 1) * slots]
-    for away in range(2, n_context):
-        pass_on(1, away)
-        if away == 2:
-            start_in(4)
-    if n_context == 2:
-        start_in(4)
+    def absorb(plane, first=False):
+        gate = jnp.zeros((n_expert * slots, hidden), jnp.float32)
+        up = gate
+        squares = jnp.zeros((n_expert * slots, 1), jnp.float32)
+        for t in range(n_tensor):
+            part = aligned((t * n_context + plane) * width, width)
+            slab = jnp.concatenate(
+                [unpacked(x_land, (seq * n_tensor + t, plane), slots, width)
+                 for seq in range(n_expert)], axis=0)
+            x_rows[:, part] = slab
+            gate = gate + dot(slab, gate_w[part, :])
+            up = up + dot(slab, up_w[part, :])
+            wide = slab.astype(jnp.float32)
+            squares = squares + jnp.sum(wide * wide, axis=1, keepdims=True)
+        gate_sum[...] = gate if first else gate_sum[...] + gate
+        up_sum[...] = up if first else up_sum[...] + up
+        inv_ref[...] = squares if first else inv_ref[...] + squares
+
+    def absorb_at(away):
+        for plane in (own_context - away, own_context + away):
+            @pl.when((plane >= 0) & (plane < n_context))
+            def _():
+                absorb(plane)
+
+    for f in range(tiles):
+        for number in range(3):
+            load(number, f).wait()
+    if n_context > 2:
+        pass_on(1, 2)
+    start_in(4)
+    absorb(own_context, True)
+    absorb_at(1)
     for f in range(tiles):
         part = slice(f * tile, (f + 1) * tile)
-        for number in range(3):
-            load(number, f).wait()
         grad_act_ref[:, part] = dot(g_rows[...], down_w[part, :], 1, 1)
-
-    for seq in range(n_expert):
-        for t in range(n_tensor):
-            for c in range(n_context):
-                at = (t * n_context + c) * width
-                x_rows[seq * slots:(seq + 1) * slots, at:at + width] = unpacked(
-                    x_land, (seq * n_tensor + t, c), slots, width)
-    x32 = x_rows[...].astype(jnp.float32)
-    inv_ref[...] = 1.0 / jnp.sqrt(
-        jnp.sum(x32 * x32, axis=1, keepdims=True) / features + EPSILON)
+    for away in range(2, n_context):
+        absorb_at(away)
+        if away + 1 < n_context:
+            pass_on(1, away + 1)
+
+    inv_ref[...] = 1.0 / jnp.sqrt(inv_ref[...] / features + EPSILON)
     inner_ref[...] = jnp.zeros_like(inner_ref)
     for f in range(tiles):
         part = slice(f * tile, (f + 1) * tile)
         inv = inv_ref[...]
-        gate = dot(x_rows[...], gate_w[:, part]) * inv
-        up = dot(x_rows[...], up_w[:, part]) * inv
+        gate = gate_sum[:, part] * inv
+        up = up_sum[:, part] * inv
         grad_act = grad_act_ref[:, part]
         sig = 1.0 / (1.0 + jnp.exp(-gate))
         grad_up = grad_act * gate * sig
@@ -670,25 +690,31 @@
 def finish_kernel(tile, x_hbm, dgate_hbm, dup_hbm, *refs):
     given, written = refs[:5], refs[5:10]
     grad_gate_hbm, grad_up_hbm, x_turned, dgate, dup, gate_out, up_out = refs[10:17]
-    load_sem, copy_sem, store_sem = refs[17:]
+    held, (load_sem, in_sem, out_sem, store_sem) = refs[17:22], refs[22:]
     loads = [pltpu.make_async_copy(src, dst, load_sem.at[i]) for i, (src, dst) in enumerate(
         ((x_hbm, x_turned), (dgate_hbm, dgate), (dup_hbm, dup)))]
-    copies = [pltpu.make_async_copy(src, dst, copy_sem.at[i])
-              for i, (src, dst) in enumerate(zip(given, written))]
-    for copy in loads + copies:
+    ins = [pltpu.make_async_copy(src, dst, in_sem.at[i])
+           for i, (src, dst) in enumerate(zip(given, held))]
+    outs = [pltpu.make_async_copy(src, dst, out_sem.at[i])
+            for i, (src, dst) in enumerate(zip(held, written))]
+    for copy in loads + ins:
         copy.start()
     for copy in loads:
         copy.wait()
-    stores = []
-    for f in range(dgate.shape[1] // tile):
+    tiles = dgate.shape[1] // tile
+    for f in range(tiles):
         part = slice(f * tile, (f + 1) * tile)
         for number, (rows_ref, out, hbm) in enumerate(
                 ((dgate, gate_out, grad_gate_hbm), (dup, up_out, grad_up_hbm))):
             out[:, part] = dot(x_turned[...], rows_ref[:, part]).astype(jnp.bfloat16)
-            stores.append(pltpu.make_async_copy(
+            outs.append(pltpu.make_async_copy(
                 out.at[:, part], hbm.at[0, :, part], store_sem.at[number, f]))
-            stores[-1].start()
-    for copy in copies + stores:
+            outs[-1].start()
+        if f == 0:
+            for i, copy in enumerate(ins):
+                copy.wait()
+                outs[i].start()
+    for copy in outs:
         copy.wait()
 
 
@@ -745,6 +771,8 @@
             scratch(features, hidden),
             scratch(hidden, features),
             scratch(routed, hidden),
+            scratch(routed, hidden, dtype=f32),
+            scratch(routed, hidden, dtype=f32),
             scratch(routed, hidden, dtype=f32),
             scratch(routed, 1, dtype=f32),
             scratch(routed, 1, dtype=f32),
@@ -775,7 +803,8 @@
         scratch_shapes=[
             scratch(features, routed), scratch(routed, hidden), scratch(routed, hidden),
             scratch(features, hidden), scratch(features, hidden),
-            dma((3,)), dma((5,)), dma((2, tiles))],
+            *[scratch(rows, local)] * 4, scratch(*down_weight.shape),
+            dma((3,)), dma((5,)), dma((5,)), dma((2, tiles))],
         compiler_params=pltpu.CompilerParams(vmem_limit_bytes=60 << 20),
     )(x_turned, dgate, dup, *small, down_grad)
     return (*small, gate_grad, up_grad, down_grad)

time: 291 us -> 135 us (0.46)
  Pallas kernels: 289 us -> 133 us
    pallas_call x1, Pallas kernels: 160 us -> 8.43 us  [by_heads(): pl.pallas_call(functools.partial(finish_kernel, tile), out_shape=[shape(r...]
    pallas_call x1, Pallas kernels: 129 us -> 125 us  [by_heads(): pl.pallas_call(functools.partial(layer_kernel, sizes, rows, capacity, slo...]
where the time goes in v4:
time: 135 us
  Pallas kernels  133 us (99%)
    pallas_call x1, Pallas kernels, by_heads(): pl.pallas_call(functools.partial(layer_kernel, sizes, rows, capacity, slo...  125 us
    pallas_call x1, Pallas kernels, by_heads(): pl.pallas_call(functools.partial(finish_kernel, tile), out_shape=[shape(r...  8.43 us

profile of v4, /device:TPU:0, one launch (start us, length us, event | category | flops | bytes accessed | tf_op | source)
XLA Modules:
  0.0 135.3 jit_solution(4909411181407181484)
XLA Ops:
  0.6 1.2 broadcast_in_dim.8.ids_ref
  1.9 124.8 %shard_map.144 = (bf16[128,1024]{1,0:T(8,128)(2,1)}, bf16[128,1024]{1,0:T(8,128)(2,1)}, bf16[128,1024]{1,0:T(8,128)(2,1)}, bf16[128,1024]{1,0:T(8,128)(2,1)}, bf...) custom-call(s32[8,128]{1,0:T(8,128)} %broadcast_in_dim.8.ids_ref, ...), custom_call_target="tpu_custom_call" | custom-call | tf_op jit(solution)/shard_map/pallas_call | solution.py:751
  126.7 8.4 %shard_map.145 = (bf16[128,1024]{1,0:T(8,128)(2,1)}, bf16[128,1024]{1,0:T(8,128)(2,1)}, bf16[128,1024]{1,0:T(8,128)(2,1)}, bf16[128,1024]{1,0:T(8,128)(2,1)}, bf...) custom-call(bf16[2048,288]{1,0:T(8,128)(2,1)} %get-tuple-element.22.x_hbm, ...), custom_call_target="tpu_custom_call" | custom-call | tf_op jit(solution)/shard_map/pallas_call | solution.py:797

commit v5 on v4

--- a/solution.py
+++ b/solution.py
@@ -483,10 +483,10 @@
     for f in range(tiles):
         for number in range(3):
             load(number, f).wait()
+    absorb(own_context, True)
     if n_context > 2:
         pass_on(1, 2)
     start_in(4)
-    absorb(own_context, True)
     absorb_at(1)
     for f in range(tiles):
         part = slice(f * tile, (f + 1) * tile)
@@ -697,10 +697,12 @@
            for i, (src, dst) in enumerate(zip(given, held))]
     outs = [pltpu.make_async_copy(src, dst, out_sem.at[i])
             for i, (src, dst) in enumerate(zip(held, written))]
-    for copy in loads + ins:
+    for copy in loads:
         copy.start()
     for copy in loads:
         copy.wait()
+    for copy in ins:
+        copy.start()
     tiles = dgate.shape[1] // tile
     for f in range(tiles):
         part = slice(f * tile, (f + 1) * tile)

time: 135 us -> 137 us (1.015)
  Pallas kernels: 133 us -> 135 us
    pallas_call x1, Pallas kernels: 8.43 us -> 9.85 us  [by_heads(): pl.pallas_call(functools.partial(finish_kernel, tile), out_shape=[shape(r...]
where the time goes in v5:
time: 137 us
  Pallas kernels  135 us (99%)
    pallas_call x1, Pallas kernels, by_heads(): pl.pallas_call(functools.partial(layer_kernel, sizes, rows, capacity, slo...  125 us
    pallas_call x1, Pallas kernels, by_heads(): pl.pallas_call(functools.partial(finish_kernel, tile), out_shape=[shape(r...  9.85 us

profile of v5, /device:TPU:0, one launch (start us, length us, event | category | flops | bytes accessed | tf_op | source)
XLA Modules:
  0.0 136.7 jit_solution(1639640329784645523)
XLA Ops:
  0.6 1.2 broadcast_in_dim.8.ids_ref
  1.9 124.8 %shard_map.144 = (bf16[128,1024]{1,0:T(8,128)(2,1)}, bf16[128,1024]{1,0:T(8,128)(2,1)}, bf16[128,1024]{1,0:T(8,128)(2,1)}, bf16[128,1024]{1,0:T(8,128)(2,1)}, bf...) custom-call(s32[8,128]{1,0:T(8,128)} %broadcast_in_dim.8.ids_ref, ...), custom_call_target="tpu_custom_call" | custom-call | tf_op jit(solution)/shard_map/pallas_call | solution.py:753
  126.7 9.8 %shard_map.145 = (bf16[128,1024]{1,0:T(8,128)(2,1)}, bf16[128,1024]{1,0:T(8,128)(2,1)}, bf16[128,1024]{1,0:T(8,128)(2,1)}, bf16[128,1024]{1,0:T(8,128)(2,1)}, bf...) custom-call(bf16[2048,288]{1,0:T(8,128)(2,1)} %get-tuple-element.22.x_hbm, ...), custom_call_target="tpu_custom_call" | custom-call | tf_op jit(solution)/shard_map/pallas_call | solution.py:799
